TPU v7x, 256 devices: a whole 4x4x8 slice. The times are simulated.
256 devices in a mesh: dp: 4 (over x_lo, core), expert: 64 (over y, x_hi, z).
Axes of the slice: x: 4 (x_hi: 2, x_lo: 2; x = x_hi * 2 + x_lo), y: 4, z: 8, core: 2. Of those that a mesh axis runs over, the one named last changes fastest.
Arguments:
- tokens: bfloat16 [512, 256, 1280], P(('dp', 'expert')), may hold values from -48 to 48
- cotangent: bfloat16 [512, 256, 1280], P(('dp', 'expert')), may hold values from -6 to 6
- router: bfloat16 [1280, 64], replicated, may hold values from -1 to 1
- first_weight: bfloat16 [64, 1280, 2560], P('expert', None, 'dp'), may hold values from -0.15625 to 0.15625
- second_weight: bfloat16 [64, 2560, 1280], P('expert', 'dp'), may hold values from -0.125 to 0.125
Outputs:
- token_grad: bfloat16 [512, 256, 1280], P(('dp', 'expert'))
- router_grad: float32 [1280, 64], P(None, 'expert')
- first_grad: bfloat16 [64, 1280, 2560], P('expert', None, 'dp')
- second_grad: bfloat16 [64, 2560, 1280], P('expert', 'dp')
All inputs are finite; a program needn't handle non-finite values.
Results may differ from a plain program's by a relative error of at most 0.018.
Values may be sent and summed in bfloat16 or wider, within the bound.
A program may use at most 128 MiB of HBM per device.

v0:
```python
import jax
import jax.numpy as jnp
from jax import lax
from jax.sharding import PartitionSpec as P

ROOT_TWO_OVER_PI = 0.7978845608028654
CUBIC_TERM = 0.044715


def gelu_value(pre_act):
    argument = ROOT_TWO_OVER_PI * (pre_act + CUBIC_TERM * pre_act * pre_act * pre_act)
    return 0.5 * pre_act * (1.0 + jnp.tanh(argument))


def gelu_slope(pre_act):
    argument = ROOT_TWO_OVER_PI * (pre_act + CUBIC_TERM * pre_act * pre_act * pre_act)
    tangent = jnp.tanh(argument)
    return 0.5 * (1.0 + tangent) + 0.5 * pre_act * (1.0 - tangent * tangent) * ROOT_TWO_OVER_PI * (
        1.0 + 3.0 * CUBIC_TERM * pre_act * pre_act
    )


def matmul(left, right):
    return jnp.dot(left, right, preferred_element_type=jnp.float32)


def matmul_nt(left, right):
    return lax.dot_general(
        left, right, (((1,), (1,)), ((), ())), preferred_element_type=jnp.float32
    )


def matmul_tn(left, right):
    return lax.dot_general(
        left, right, (((0,), (0,)), ((), ())), preferred_element_type=jnp.float32
    )


def send_grads(slot_grad, model_width):
    arrived = lax.all_to_all(slot_grad, "expert", split_axis=1, concat_axis=0, tiled=True)
    return arrived.reshape(-1, model_width)


def body(tokens, cotangent, router, first_weight, second_weight):
    image_count = tokens.shape[0]
    model_width = tokens.shape[2]
    expert_count = lax.axis_size("expert")
    logits = jnp.einsum("imd,de->ime", tokens, router, preferred_element_type=jnp.float32)
    dispatch = jax.nn.softmax(logits, axis=1)
    combine = jax.nn.softmax(logits, axis=2)
    dispatch_low = dispatch.astype(jnp.bfloat16)
    combine_low = combine.astype(jnp.bfloat16)
    slot_in = jnp.einsum(
        "ime,imd->ied", dispatch_low, tokens, preferred_element_type=jnp.float32
    ).astype(jnp.bfloat16)
    slot_grad = jnp.einsum(
        "ime,imd->ied", combine_low, cotangent, preferred_element_type=jnp.float32
    ).astype(jnp.bfloat16)
    mine_grad = None
    mine_in = lax.all_to_all(slot_in, "expert", split_axis=1, concat_axis=0, tiled=True).reshape(
        -1, model_width
    )
    mine_grad = send_grads(slot_grad, model_width)
    every_in, every_grad = (
        lax.all_gather(mine_in, "dp", axis=0, tiled=True),
        lax.all_gather(mine_grad, "dp", axis=0, tiled=True),
    )
    w_first = first_weight[0]
    w_second = second_weight[0]
    pre_act = matmul(every_in, w_first)
    hidden_act = gelu_value(pre_act).astype(jnp.bfloat16)
    act_grad = matmul_nt(every_grad, w_second)
    pre_grad = (act_grad * gelu_slope(pre_act)).astype(jnp.bfloat16)
    grad_first = matmul_tn(every_in, pre_grad)
    grad_second = matmul_tn(hidden_act, every_grad)
    forward_part = matmul(hidden_act, w_second)
    backward_part = matmul_nt(pre_grad, w_first)
    summed = lax.psum_scatter(
        jnp.concatenate([forward_part, backward_part], axis=1).astype(jnp.bfloat16),
        "dp",
        scatter_dimension=0,
        tiled=True,
    ).astype(jnp.float32)
    slot_out = summed[:, :model_width].astype(jnp.bfloat16)
    slot_back = summed[:, model_width:].astype(jnp.bfloat16)
    shaped_out = slot_out.reshape(expert_count, image_count, 1, model_width)
    shaped_back = slot_back.reshape(expert_count, image_count, 1, model_width)
    back_out, back_grad = (
        lax.all_to_all(shaped_out, "expert", split_axis=0, concat_axis=2, tiled=True),
        lax.all_to_all(shaped_back, "expert", split_axis=0, concat_axis=2, tiled=True),
    )
    expert_out = back_out.reshape(image_count, expert_count, model_width)
    expert_back = back_grad.reshape(image_count, expert_count, model_width)
    combine_grad = jnp.einsum(
        "imd,ied->ime", cotangent, expert_out, preferred_element_type=jnp.float32
    )
    dispatch_grad = jnp.einsum(
        "imd,ied->ime", tokens, expert_back, preferred_element_type=jnp.float32
    )
    logit_grad = dispatch * (
        dispatch_grad - jnp.sum(dispatch * dispatch_grad, axis=1, keepdims=True)
    )
    logit_grad = logit_grad + combine * (
        combine_grad - jnp.sum(combine * combine_grad, axis=2, keepdims=True)
    )
    logit_low = logit_grad.astype(jnp.bfloat16)
    token_part = jnp.einsum(
        "ime,ied->imd", dispatch_low, expert_back, preferred_element_type=jnp.float32
    )
    token_part = token_part + jnp.einsum(
        "ime,de->imd", logit_low, router, preferred_element_type=jnp.float32
    )
    token_grad = token_part.astype(jnp.bfloat16)
    router_part = jnp.einsum("imd,ime->de", tokens, logit_low, preferred_element_type=jnp.float32)
    router_column = lax.psum_scatter(router_part, "expert", scatter_dimension=1, tiled=True)
    router_grad = lax.psum(router_column, "dp")
    return (
        token_grad,
        router_grad,
        grad_first[None].astype(jnp.bfloat16),
        grad_second[None].astype(jnp.bfloat16),
    )


def solution(mesh):
    placed = (
        P(("dp", "expert"), None, None),
        P(("dp", "expert"), None, None),
        P(),
        P("expert", None, "dp"),
        P("expert", "dp", None),
    )
    return jax.shard_map(
        body,
        mesh=mesh,
        in_specs=placed,
        out_specs=(
            P(("dp", "expert"), None, None),
            P(None, "expert"),
            P("expert", None, "dp"),
            P("expert", "dp", None),
        ),
        check_vma=False,
    )
```

profile of v0, /device:TPU:1, one launch (start us, length us, event | category | flops | bytes accessed | tf_op | source)
XLA Modules:
  0.0 852.5 jit_solution(6657359294390855553)
XLA Ops:
  7.2 2.0 fusion.46
  10.7 29.0 %all_to_all.60 = bf16[2,64,1280]{2,0,1:T(2,128)(2,1)S(1)} all-to-all(bf16[2,64,1280]{2,0,1:T(2,128)(2,1)S(1)} %copy.15), channel_id=1, replica_groups=mesh['dp'=4,'expert'=64] {'expert'}, dimensions={1} | all-to-all | bytes 655360 | tf_op jit(solution)/shard_map/all_to_all | solution.py:60
  43.4 19.4 %all_to_all.61 = bf16[2,64,1280]{2,0,1:T(2,128)(2,1)S(1)} all-to-all(bf16[2,64,1280]{2,0,1:T(2,128)(2,1)S(1)} %copy.16), channel_id=1, replica_groups=mesh['dp'=4,'expert'=64] {'expert'}, dimensions={1} | all-to-all | bytes 655360 | tf_op jit(solution)/shard_map/all_to_all | solution.py:40
  63.8 1.7 all-gather.3.cloned.1.call-done
  65.5 3.0 fusion.11
  69.6 2.5 convolution_convert_fusion.3
  72.0 22.4 %all-gather.5.cloned.1.call-done = bf16[512,1280]{1,0:T(8,128)(2,1)} async-done(((bf16[128,1280]{1,0:T(8,128)(2,1)}), bf16[512,1280]{1,0:T(8,128)(2,1)}) %all-gather.5.cloned.1.call-update) | async-done | bytes 1310736 | tf_op jit(solution)/shard_map/all_gather | solution.py:66
  94.4 3.4 fusion.16
  100.0 1.7 pad_maximum_fusion
  101.8 36.0 %reduce-scatter.2.cloned.1.call-done = bf16[128,2560]{1,0:T(8,128)(2,1)} async-done(((bf16[512,2560]{1,0:T(8,128)(2,1)}), bf16[128,2560]{1,0:T(8,128)(2,1)}) %reduce-scatter.2.cloned.1.call-update) | async-done | bytes 655376 | tf_op jit(solution)/shard_map/reduce_scatter | solution.py:78
  137.8 1.8 fusion.54
  140.5 12.3 %all-to-all-start.2 = ((bf16[64,2,1,1280]{3,1,2,0:T(2,128)(2,1)}), bf16[64,2,1,1280]{3,1,2,0:T(2,128)(2,1)S(1)}, u32[]{:S(2)}, u32[]{:S(2)}) async-start(bf16[64,2,1,1280]{3,1,2,0:T(2,128)(2,1)} %bitcast.77), calls=%async_computation.3 | async-start | bytes 655360 | tf_op jit(solution)/shard_map/all_to_all | solution.py:90
  153.4 4.0 fusion.6
  157.4 1.8 reshape.42
  159.2 8.2 all-to-all-done.2
  167.4 6.0 all-to-all-start.3
  173.6 3.9 fusion.5
  178.8 7.8 all-to-all-done.3
  186.6 2.6 convolution_bitcast_fusion.1
  189.2 2.2 convolution_bitcast_fusion
  191.4 2.2 fusion.36
  193.6 3.6 fusion.4
  197.2 608.6 %all-reduce.3.cloned.1.call-done = f32[1280,64]{0,1:T(8,128)} async-done(((f32[1280,64]{0,1:T(8,128)}), f32[1280,64]{0,1:T(8,128)}) %all-reduce.3.cloned.1.call-update) | async-done | bytes 327696
  807.3 38.7 %psum.7 = f32[1280,1]{0,1:T(1,128)} all-reduce(f32[1280,1]{0,1:T(1,128)S(1)} %constant_dynamic-slice_fusion), channel_id=1, replica_groups=mesh['dp'=4,'expert'=64] {'dp'}, use_global_device_ids=true, to_apply=%region_8.0 | all-reduce | flops 1280 | bytes 10240 | tf_op jit(solution)/shard_map/psum | solution.py:116
  (40 shorter events, 13.7 us)
Async XLA Ops:
  7.2 62.4 %copy-start = (bf16[1,640,1280]{2,1,0:T(8,128)(2,1)S(1)}, bf16[1,640,1280]{2,1,0:T(8,128)(2,1)}, u32[]{:S(2)}) copy-start(bf16[1,640,1280]{2,1,0:T(8,128)(2,1)} %param.9) | copy-start | bytes 4915204
  7.2 2.8 copy-start.1
  7.2 58.3 %all-gather.3.cloned.1.call-start = ((), (), s32[]{:S(2)}) async-start(), calls=%async_computation.5 | async-start | bytes 1638400 | tf_op jit(solution)/shard_map/all_gather | solution.py:65
  40.6 53.8 %all-gather.5.cloned.1.call-start = ((), (), s32[]{:S(2)}) async-start(), calls=%async_computation.6 | async-start | bytes 1638400 | tf_op jit(solution)/shard_map/all_gather | solution.py:66
  63.7 74.1 %reduce-scatter.2.cloned.1.call-start = ((), (), s32[]{:S(2)}) async-start(), calls=%async_computation.7 | async-start | bytes 3276800 | tf_op jit(solution)/shard_map/reduce_scatter | solution.py:78
  68.5 1.1 copy-start.8
  94.4 4.3 copy-start.5
  97.9 0.9 copy-start.7
  98.7 1.3 copy-start.2
  101.8 51.0 %copy-start.6 = (u32[256]{0:T(256)S(1)}, u32[256]{0:T(256)}, u32[]{:S(2)}) copy-start(u32[256]{0:T(256)} %constant.22) | copy-start | bytes 3076
  140.5 26.9 %all-to-all-start.2 = ((bf16[64,2,1,1280]{3,1,2,0:T(2,128)(2,1)}), bf16[64,2,1,1280]{3,1,2,0:T(2,128)(2,1)S(1)}, u32[]{:S(2)}, u32[]{:S(2)}) async-start(bf16[64,2,1,1280]{3,1,2,0:T(2,128)(2,1)} %bitcast.77), calls=%async_computation.3 | async-start | bytes 655360 | tf_op jit(solution)/shard_map/all_to_all | solution.py:90
  167.4 19.2 %all-to-all-start.3 = ((bf16[64,2,1,1280]{3,1,2,0:T(2,128)(2,1)}), bf16[64,2,1,1280]{3,1,2,0:T(2,128)(2,1)}, u32[]{:S(2)}, u32[]{:S(2)}) async-start(bf16[64,2,1,1280]{3,1,2,0:T(2,128)(2,1)} %bitcast.78), calls=%async_computation.4 | async-start | bytes 655360 | tf_op jit(solution)/shard_map/all_to_all | solution.py:89
  173.4 632.4 %all-reduce.3.cloned.1.call-start = ((), (), s32[]{:S(2)}) async-start(), calls=%async_computation.8 | async-start | bytes 655360
  177.5 0.9 copy-start.4
  191.4 2.2 copy-start.3
Sparse Core Ops, SparseCore 0:
  40.8 24.6 all-gather.2
  67.9 26.5 all-gather.4
  101.9 35.8 reduce-scatter.1
  191.5 614.2 all-reduce.2
where the time goes:
time: 853 us; the launch traced here: 852 us
  waiting for transfers between devices  685 us (80%)
  blocking collectives  87.2 us (10%)
  matrix products  33.1 us (4%)
  starting transfers between devices  18.6 us (2%)
  between operations  13.9 us (2%)
  local copies, waits for them, and re-layouts  11.3 us (1%)
    unnamed x5, waiting for transfers between devices  609 us
    psum x1, blocking collectives, body(): router_grad = lax.psum(router_column, 'dp')  38.7 us
    reduce_scatter x1, waiting for transfers between devices, body(): lax.psum_scatter(jnp.concatenate([forward_part, backward_part], axis=1).a...  36 us
    all_to_all x1, blocking collectives, body(): lax.all_to_all(slot_in, 'expert', split_axis=1, concat_axis=0, tiled=True)  29 us
    all_gather x1, waiting for transfers between devices, body(): lax.all_gather(mine_grad, 'dp', axis=0, tiled=True)  22.4 us
    all_to_all x1, blocking collectives, send_grads(): lax.all_to_all(slot_grad, 'expert', split_axis=1, concat_axis=0, tiled=True)  19.4 us
  transfers between devices with their start and end apart: 6, of which 6 were waited for; matrix products, arithmetic and copies ran while one was open for 3% of the time, Pallas kernels for 0%

commit v1 on v0

--- a/solution.py
+++ b/solution.py
@@ -111,9 +111,9 @@
         "ime,de->imd", logit_low, router, preferred_element_type=jnp.float32
     )
     token_grad = token_part.astype(jnp.bfloat16)
-    router_part = jnp.einsum("imd,ime->de", tokens, logit_low, preferred_element_type=jnp.float32)
-    router_column = lax.psum_scatter(router_part, "expert", scatter_dimension=1, tiled=True)
-    router_grad = lax.psum(router_column, "dp")
+    router_part = jnp.einsum("ime,imd->ed", logit_low, tokens, preferred_element_type=jnp.float32)
+    router_parts = lax.all_to_all(router_part, "expert", split_axis=0, concat_axis=0, tiled=True)
+    router_grad = lax.psum(jnp.sum(router_parts, axis=0), "dp")[:, None]
     return (
         token_grad,
         router_grad,

time: 853 us -> 230 us (0.27)
  waiting for transfers between devices: 685 us -> 84.3 us
  blocking collectives: 87.2 us -> 58.4 us
    unnamed x5 -> x3, waiting for transfers between devices: 609 us -> 0.05 us
    psum x1, blocking collectives: 38.7 us -> 9.93 us  [body(): router_grad = lax.psum(jnp.sum(router_parts, axis=0), 'dp')[:, None]]
  transfers between devices with their start and end apart: 6 -> 6, of which waited for: 6 -> 6; matrix products, arithmetic and copies ran while one was open for 3% -> 11% of each run, Pallas kernels for 0% -> 0%
where the time goes in v1:
time: 230 us; the launch traced here: 229 us
  waiting for transfers between devices  84.3 us (37%)
  blocking collectives  58.4 us (25%)
  matrix products  32.9 us (14%)
  starting transfers between devices  24.7 us (11%)
  between operations  13.9 us (6%)
  local copies, waits for them, and re-layouts  11.4 us (5%)
  other arithmetic  3.75 us (2%)
    reduce_scatter x1, waiting for transfers between devices, body(): lax.psum_scatter(jnp.concatenate([forward_part, backward_part], axis=1).a...  36 us
    all_to_all x1, blocking collectives, body(): lax.all_to_all(slot_in, 'expert', split_axis=1, concat_axis=0, tiled=True)  29.1 us
    all_gather x1, waiting for transfers between devices, body(): lax.all_gather(mine_grad, 'dp', axis=0, tiled=True)  22.4 us
    all_to_all x1, blocking collectives, send_grads(): lax.all_to_all(slot_grad, 'expert', split_axis=1, concat_axis=0, tiled=True)  19.4 us
    all_to_all x1, waiting for transfers between devices, body(): lax.all_to_all(shaped_back, 'expert', split_axis=0, concat_axis=2, tiled=...  12.8 us
    all_to_all x1, starting transfers between devices, body(): lax.all_to_all(shaped_back, 'expert', split_axis=0, concat_axis=2, tiled=...  12.3 us
    psum x1, blocking collectives, body(): router_grad = lax.psum(jnp.sum(router_parts, axis=0), 'dp')[:, None]  9.93 us
    all_to_all x1, waiting for transfers between devices, body(): lax.all_to_all(shaped_out, 'expert', split_axis=0, concat_axis=2, tiled=T...  7.73 us
  transfers between devices with their start and end apart: 6, of which 6 were waited for; matrix products, arithmetic and copies ran while one was open for 11% of the time, Pallas kernels for 0%

profile of v1, /device:TPU:1, one launch (start us, length us, event | category | flops | bytes accessed | tf_op | source)
XLA Modules:
  0.0 229.3 jit_solution(12086264263127764922)
XLA Ops:
  7.2 2.0 fusion.46
  10.7 29.1 %all_to_all.69 = bf16[2,64,1280]{2,0,1:T(2,128)(2,1)S(1)} all-to-all(bf16[2,64,1280]{2,0,1:T(2,128)(2,1)S(1)} %copy.15), channel_id=1, replica_groups=mesh['dp'=4,'expert'=64] {'expert'}, dimensions={1} | all-to-all | bytes 655360 | tf_op jit(solution)/shard_map/all_to_all | solution.py:60
  43.4 19.4 %all_to_all.70 = bf16[2,64,1280]{2,0,1:T(2,128)(2,1)S(1)} all-to-all(bf16[2,64,1280]{2,0,1:T(2,128)(2,1)S(1)} %copy.16), channel_id=1, replica_groups=mesh['dp'=4,'expert'=64] {'expert'}, dimensions={1} | all-to-all | bytes 655360 | tf_op jit(solution)/shard_map/all_to_all | solution.py:40
  65.5 3.0 %fusion.11 = f32[512,640]{1,0:T(8,128)S(1)} fusion(bf16[512,1280]{1,0:T(8,128)(2,1)} %all-gather.3.cloned.1.call-done, bf16[1,1280,640]{2,1,0:T(8,128)(2,1)} %param.8), kind=kOutput, calls=%fused_computation.22 | convolution fusion | flops 838860800 | bytes 4259840 | tf_op jit(solution)/shard_map/dot_general | solution.py:24
  69.6 2.5 %convolution_convert_fusion.3 = bf16[512,1280]{1,0:T(8,128)(2,1)} fusion(bf16[1,640,1280]{2,1,0:T(8,128)(2,1)S(1)} %copy-done, f32[512,640]{1,0:T(8,128)S(1)} %fusion.11), kind=kOutput, calls=%fused_computation.8 | convolution fusion | flops 842465280 | bytes 4259840 | tf_op jit(solution)/shard_map/dot_general | solution.py:24
  72.0 22.4 %all-gather.5.cloned.1.call-done = bf16[512,1280]{1,0:T(8,128)(2,1)} async-done(((bf16[128,1280]{1,0:T(8,128)(2,1)}), bf16[512,1280]{1,0:T(8,128)(2,1)}) %all-gather.5.cloned.1.call-update) | async-done | bytes 1310736 | tf_op jit(solution)/shard_map/all_gather | solution.py:66
  94.4 3.4 %fusion.16 = bf16[512,640]{1,0:T(8,128)(2,1)S(1)} fusion(bf16[512,1280]{1,0:T(8,128)(2,1)} %all-gather.5.cloned.1.call-done, bf16[1,640,1280]{2,1,0:T(8,128)(2,1)S(1)} %copy-done, f32[512,640]{1,0:T(8,128)} %copy-done.8), kind=kOutput, calls=%fused_computation.25 | convolution fusion | flops 845086720 | bytes 4915200 | tf_op jit(solution)/shard_map/dot_general | solution.py:28
  101.7 36.0 %reduce-scatter.2.cloned.1.call-done = bf16[128,2560]{1,0:T(8,128)(2,1)} async-done(((bf16[512,2560]{1,0:T(8,128)(2,1)}), bf16[128,2560]{1,0:T(8,128)(2,1)}) %reduce-scatter.2.cloned.1.call-update) | async-done | bytes 655376 | tf_op jit(solution)/shard_map/reduce_scatter | solution.py:78
  137.8 1.8 fusion.54
  140.4 12.3 %all-to-all-start.2 = ((bf16[64,2,1,1280]{3,1,2,0:T(2,128)(2,1)}), bf16[64,2,1,1280]{3,1,2,0:T(2,128)(2,1)S(1)}, u32[]{:S(2)}, u32[]{:S(2)}) async-start(bf16[64,2,1,1280]{3,1,2,0:T(2,128)(2,1)} %bitcast.76), calls=%async_computation.3 | async-start | bytes 655360 | tf_op jit(solution)/shard_map/all_to_all | solution.py:90
  152.8 1.8 reshape.44
  154.6 12.8 %all-to-all-done.2 = bf16[64,2,1,1280]{3,1,2,0:T(2,128)(2,1)S(1)} async-done(((bf16[64,2,1,1280]{3,1,2,0:T(2,128)(2,1)}), bf16[64,2,1,1280]{3,1,2,0:T(2,128)(2,1)S(1)}, u32[]{:S(2)}, u32[]{:S(2)}) %all-to-all-start.2) | async-done | bytes 327712 | tf_op jit(solution)/shard_map/all_to_all | solution.py:90
  167.4 6.2 %all-to-all-start.3 = ((bf16[64,2,1,1280]{3,1,2,0:T(2,128)(2,1)}), bf16[64,2,1,1280]{3,1,2,0:T(2,128)(2,1)}, u32[]{:S(2)}, u32[]{:S(2)}) async-start(bf16[64,2,1,1280]{3,1,2,0:T(2,128)(2,1)} %bitcast.75), calls=%async_computation.4 | async-start | bytes 655360 | tf_op jit(solution)/shard_map/all_to_all | solution.py:89
  173.6 4.0 %fusion.6 = bf16[1,640,1280]{2,1,0:T(8,128)(2,1)} fusion(bf16[512,1280]{1,0:T(8,128)(2,1)} %all-gather.5.cloned.1.call-done, f32[512,640]{1,0:T(8,128)} %copy-done.8), kind=kOutput, calls=%fused_computation.11 | convolution fusion | flops 842629120 | bytes 4259840 | tf_op jit(solution)/shard_map/dot_general | solution.py:34
  178.9 7.7 %all-to-all-done.3 = bf16[64,2,1,1280]{3,1,2,0:T(2,128)(2,1)} async-done(((bf16[64,2,1,1280]{3,1,2,0:T(2,128)(2,1)}), bf16[64,2,1,1280]{3,1,2,0:T(2,128)(2,1)}, u32[]{:S(2)}, u32[]{:S(2)}) %all-to-all-start.3) | async-done | bytes 327712 | tf_op jit(solution)/shard_map/all_to_all | solution.py:89
  186.6 2.6 %convolution_bitcast_fusion.1 = f32[2,256,64]{1,2,0:T(8,128)} fusion(bf16[2,256,1280]{2,1,0:T(8,128)(2,1)} %param.6, bf16[64,2,1,1280]{3,1,2,0:T(2,128)(2,1)} %all-to-all-done.3), kind=kOutput, calls=%fused_computation.41 | convolution fusion | flops 83886080 | bytes 1769472 | tf_op jit(solution)/shard_map/imd,ied->ime/dot_general | solution.py:94
  189.2 2.2 convolution_bitcast_fusion
  191.4 2.1 copy.21
  193.5 6.1 %all-to-all-start.4 = ((f32[64,1,1280]{2,1,0:T(1,128)}), f32[64,1,1280]{2,1,0:T(1,128)S(1)}, u32[]{:S(2)}, u32[]{:S(2)}) async-start(f32[64,1,1280]{2,1,0:T(1,128)} %copy.21), calls=%async_computation.5 | async-start | bytes 655360 | tf_op jit(solution)/shard_map/all_to_all | solution.py:115
  199.6 3.7 %fusion.5 = bf16[1,1280,640]{2,1,0:T(8,128)(2,1)} fusion(bf16[512,1280]{1,0:T(8,128)(2,1)} %all-gather.3.cloned.1.call-done, bf16[512,640]{1,0:T(8,128)(2,1)S(1)} %copy-done.7), kind=kOutput, calls=%fused_computation.10 | convolution fusion | flops 839680000 | bytes 3604480 | tf_op jit(solution)/shard_map/dot_general | solution.py:34
  203.3 2.2 fusion.36
  205.5 3.6 %fusion.4 = bf16[2,256,1280]{2,1,0:T(8,128)(2,1)} fusion(f32[2,256,1280]{2,1,0:T(8,128)} %fusion.36, f32[2,256,64]{1,2,0:T(8,128)S(1)} %fusion.32, f32[2,256,64]{1,2,0:T(8,128)} %convolution_bitcast_fusion.1, bf16[1280,64]{0,1:T(8,128)(2,1)S(1)} %copy-done.3, f32[2,256,64]{1,2,0:T(8,128)} %get-tuple-element.7, f32[2,256]{1,0:T(2,128)S(1)} %get-tuple-element.6), kind=kOutput, calls=%fused_computation.9 | convolution fusion | flops 85426752 | bytes 4491264 | tf_op jit(solution)/shard_map/ime,de->imd/dot_general | solution.py:110
  209.1 3.5 %all-to-all-done.4 = f32[64,1,1280]{2,1,0:T(1,128)S(1)} async-done(((f32[64,1,1280]{2,1,0:T(1,128)}), f32[64,1,1280]{2,1,0:T(1,128)S(1)}, u32[]{:S(2)}, u32[]{:S(2)}) %all-to-all-start.4) | async-done | bytes 327712 | tf_op jit(solution)/shard_map/all_to_all | solution.py:115
  212.9 9.9 %psum.7 = f32[1280,1]{0,1:T(1,128)} all-reduce(f32[1280,1]{0,1:T(1,128)S(1)} %broadcast_in_dim.2), channel_id=1, replica_groups=mesh['dp'=4,'expert'=64] {'dp'}, use_global_device_ids=true, to_apply=%region_8.0 | all-reduce | flops 1280 | bytes 10240 | tf_op jit(solution)/shard_map/psum | solution.py:116
  (40 shorter events, 15.0 us)
Async XLA Ops:
  7.2 62.4 %copy-start = (bf16[1,640,1280]{2,1,0:T(8,128)(2,1)S(1)}, bf16[1,640,1280]{2,1,0:T(8,128)(2,1)}, u32[]{:S(2)}) copy-start(bf16[1,640,1280]{2,1,0:T(8,128)(2,1)} %param.9) | copy-start | bytes 4915204
  7.2 2.8 %copy-start.1 = (bf16[2,256,1280]{2,1,0:T(8,128)(2,1)S(1)}, bf16[2,256,1280]{2,1,0:T(8,128)(2,1)}, u32[]{:S(2)}) copy-start(bf16[2,256,1280]{2,1,0:T(8,128)(2,1)} %param.5) | copy-start | bytes 3932164
  7.2 58.3 %all-gather.3.cloned.1.call-start = ((), (), s32[]{:S(2)}) async-start(), calls=%async_computation.6 | async-start | bytes 1638400 | tf_op jit(solution)/shard_map/all_gather | solution.py:65
  40.6 53.8 %all-gather.5.cloned.1.call-start = ((), (), s32[]{:S(2)}) async-start(), calls=%async_computation.7 | async-start | bytes 1638400 | tf_op jit(solution)/shard_map/all_gather | solution.py:66
  63.7 74.1 %reduce-scatter.2.cloned.1.call-start = ((), (), s32[]{:S(2)}) async-start(), calls=%async_computation.8 | async-start | bytes 3276800 | tf_op jit(solution)/shard_map/reduce_scatter | solution.py:78
  68.5 1.1 copy-start.8
  94.4 4.3 %copy-start.5 = (bf16[1,1280,640]{2,1,0:T(8,128)(2,1)S(1)}, bf16[1,1280,640]{2,1,0:T(8,128)(2,1)}, u32[]{:S(2)}) copy-start(bf16[1,1280,640]{2,1,0:T(8,128)(2,1)} %param.8) | copy-start | bytes 4915204
  97.9 0.8 copy-start.6
  98.7 1.3 copy-start.2
  140.4 27.0 %all-to-all-start.2 = ((bf16[64,2,1,1280]{3,1,2,0:T(2,128)(2,1)}), bf16[64,2,1,1280]{3,1,2,0:T(2,128)(2,1)S(1)}, u32[]{:S(2)}, u32[]{:S(2)}) async-start(bf16[64,2,1,1280]{3,1,2,0:T(2,128)(2,1)} %bitcast.76), calls=%async_computation.3 | async-start | bytes 655360 | tf_op jit(solution)/shard_map/all_to_all | solution.py:90
  167.4 19.2 %all-to-all-start.3 = ((bf16[64,2,1,1280]{3,1,2,0:T(2,128)(2,1)}), bf16[64,2,1,1280]{3,1,2,0:T(2,128)(2,1)}, u32[]{:S(2)}, u32[]{:S(2)}) async-start(bf16[64,2,1,1280]{3,1,2,0:T(2,128)(2,1)} %bitcast.75), calls=%async_computation.4 | async-start | bytes 655360 | tf_op jit(solution)/shard_map/all_to_all | solution.py:89
  177.6 0.9 copy-start.4
  191.4 8.2 %copy-start.7 = (bf16[512,640]{1,0:T(8,128)(2,1)S(1)}, bf16[512,640]{1,0:T(8,128)(2,1)}, u32[]{:S(2)}) copy-start(bf16[512,640]{1,0:T(8,128)(2,1)} %copy-done.6) | copy-start | bytes 1966084
  193.5 19.2 %all-to-all-start.4 = ((f32[64,1,1280]{2,1,0:T(1,128)}), f32[64,1,1280]{2,1,0:T(1,128)S(1)}, u32[]{:S(2)}, u32[]{:S(2)}) async-start(f32[64,1,1280]{2,1,0:T(1,128)} %copy.21), calls=%async_computation.5 | async-start | bytes 655360 | tf_op jit(solution)/shard_map/all_to_all | solution.py:115
  203.3 2.2 copy-start.3
Sparse Core Ops, SparseCore 0:
  40.8 24.6 all-gather.2
  67.9 26.5 all-gather.4
  101.9 35.8 reduce-scatter.1

commit v2 on v1

v2 whole, which is shorter than its diff:
```python
import functools

import jax
import jax.numpy as jnp
from jax import lax
from jax.experimental import pallas as pl
from jax.experimental.pallas import tpu as pltpu
from jax.sharding import PartitionSpec as P

ROOT_TWO_OVER_PI = 0.7978845608028654
CUBIC_TERM = 0.044715
MESH = pl.DeviceIdType.MESH
F32, BF16 = jnp.float32, jnp.bfloat16

NZ, NYX = 8, 8
IMG, TOK, DIM, HID, EXP = 2, 256, 1280, 640, 64
CW = 256
NC = DIM // CW
ROWS = 128
N_BLK = 4


def mm(a, b):
    return lax.dot_general(a, b, (((1,), (0,)), ((), ())), preferred_element_type=F32)


def mm_nt(a, b):
    return lax.dot_general(a, b, (((1,), (1,)), ((), ())), preferred_element_type=F32)


def mm_tn(a, b):
    return lax.dot_general(a, b, (((0,), (0,)), ((), ())), preferred_element_type=F32)


def iota(shape, axis):
    return lax.broadcasted_iota(jnp.int32, shape, axis)


def one_hot(mask):
    return jnp.where(mask, 1.0, 0.0).astype(BF16)


def kernel(
    tok_hbm, cot_hbm, rt_hbm, w1_hbm, w2_hbm,
    tg_hbm, rg_out, g1_hbm, g2_hbm,
    tok, cot, rt, w1, w2, ltm, disp, comb, dlow, perm1, perm3,
    send1, recv1, send2, xs, acc_pre, acc_act, hid, pg,
    op, rc, t_own, sx, rx, so, ry, sz, rz, rp, cg, dg, llow,
    tgv, g1v, g2v, rsend, rrecv, rs2, rr2, rs3, rr3, rs4, rr4,
    in_sem, out_sem, z1_sem, y1_sem, agx_sem, agc_sem, agd_sem,
    rc_sem, rx_sem, ry_sem, rz_sem, rt_sem, snd_sem,
):
    p = lax.axis_index("dp")
    q = lax.axis_index("expert")
    z = q % NZ
    yx = q // NZ
    y = yx // 2
    xh = yx % 2

    def z_peer(k):
        zt = (z + k) % NZ
        return zt, (p, yx * NZ + zt)

    def yx_peer(k):
        dx = k % 2
        yt = (y + k // 2) % 4
        yxt = yt * 2 + (xh + dx) % 2
        return yxt, ((p + 2 * dx) % 4, yxt * NZ + z)

    core_peer = (p + 1 - 2 * (p % 2), q)
    x_peer = ((p + 2) % 4, q)

    def remote(src, dst, send_sem, recv_sem, dev):
        pltpu.make_async_remote_copy(
            src_ref=src, dst_ref=dst, send_sem=send_sem, recv_sem=recv_sem,
            device_id=dev, device_id_type=MESH,
        ).start()

    def await_bytes(ref, sem):
        pltpu.make_async_copy(ref, ref, sem).wait()

    def cols(c):
        return pl.ds(pl.multiple_of(c * CW, CW), CW)

    loads = [
        pltpu.make_async_copy(a, b, in_sem.at[i])
        for i, (a, b) in enumerate(
            ((tok_hbm, tok), (rt_hbm, rt), (cot_hbm, cot), (w1_hbm, w1), (w2_hbm, w2))
        )
    ]
    for load in loads:
        load.start()

    barrier = pltpu.get_barrier_semaphore()

    @pl.loop(1, 8)
    def _(k):
        pl.semaphore_signal(barrier, inc=1, device_id=z_peer(k)[1], device_id_type=MESH)
        pl.semaphore_signal(barrier, inc=1, device_id=yx_peer(k)[1], device_id_type=MESH)

    pl.semaphore_signal(barrier, inc=1, device_id=core_peer, device_id_type=MESH)
    pl.semaphore_signal(barrier, inc=1, device_id=x_peer, device_id_type=MESH)

    o1, n1 = iota((256, 256), 0), iota((256, 256), 1)
    perm1[...] = one_hot(
        n1 == ((o1 >> 1) & 7) * 32 + ((o1 >> 4) & 7) * 4 + (o1 >> 7) * 2 + (o1 & 1)
    )
    perm3[...] = one_hot(
        n1 == (o1 & 7) * 32 + ((o1 >> 3) & 7) * 4 + ((o1 >> 6) & 1) * 2 + (o1 >> 7)
    )
    n2, e2 = iota((256, EXP), 0), iota((256, EXP), 1)
    same_slot = e2 == ((n2 >> 2) & 7) * 8 + (n2 >> 5)

    loads[0].wait()
    loads[1].wait()
    logits = mm(tok[...], rt[...])
    for i in range(IMG):
        rows = pl.ds(i * TOK, TOK)
        part = logits[i * TOK:(i + 1) * TOK]
        up = jnp.exp(part - jnp.max(part, axis=0, keepdims=True))
        d = up / jnp.sum(up, axis=0, keepdims=True)
        up = jnp.exp(part - jnp.max(part, axis=1, keepdims=True))
        c = up / jnp.sum(up, axis=1, keepdims=True)
        disp[rows, :] = d
        comb[rows, :] = c
        d_low = d.astype(BF16)
        dlow[rows, :] = d_low
        for a, low in ((0, d_low), (1, c.astype(BF16))):
            spread = one_hot(same_slot & ((n2 & 3) == a * 2 + i))
            ltm[:, pl.ds(a * 512 + i * TOK, TOK)] = mm_nt(spread, low).astype(BF16)
    loads[2].wait()
    pl.semaphore_wait(barrier, 16)

    def send_slots(c):
        ch = cols(c)
        send1[:, ch] = (
            mm(ltm[:, :512], tok[:, ch]) + mm(ltm[:, 512:], cot[:, ch])
        ).astype(BF16)
        mine = pl.ds(pl.multiple_of(z * 32, 32), 32)
        pltpu.make_async_copy(send1.at[mine, ch], recv1.at[mine, ch], z1_sem.at[c]).start()

        @pl.loop(1, 8)
        def _(k):
            zt, dev = z_peer(k)
            remote(
                send1.at[pl.ds(pl.multiple_of(zt * 32, 32), 32), ch], recv1.at[mine, ch],
                snd_sem.at[0], z1_sem.at[c], dev,
            )

    def turn_slots(c):
        ch = cols(c)
        await_bytes(recv1.at[:, ch], z1_sem.at[c])
        send2[:, :, ch] = mm(perm1[...], recv1[:, ch]).astype(BF16).reshape(2, ROWS, CW)
        mine = pl.ds(pl.multiple_of(yx * 16, 16), 16)
        pltpu.make_async_copy(
            send2.at[:, mine, ch], xs.at[0, :, mine, ch], y1_sem.at[c]
        ).start()

        @pl.loop(1, 8)
        def _(k):
            yxt, dev = yx_peer(k)
            remote(
                send2.at[:, pl.ds(pl.multiple_of(yxt * 16, 16), 16), ch],
                xs.at[0, :, mine, ch], snd_sem.at[1], y1_sem.at[c], dev,
            )

    def gather_slots(c):
        ch = cols(c)
        await_bytes(xs.at[0, :, :, ch], y1_sem.at[c])
        remote(xs.at[0, :, :, ch], xs.at[1, :, :, ch], snd_sem.at[2], agx_sem.at[c], x_peer)
        remote(xs.at[0, :, :, ch], xs.at[2, :, :, ch], snd_sem.at[3], agc_sem.at[c], core_peer)

    def forward_slots(c):
        ch = cols(c)
        await_bytes(xs.at[1, :, :, ch], agx_sem.at[c])
        remote(xs.at[1, :, :, ch], xs.at[3, :, :, ch], snd_sem.at[4], agd_sem.at[c], core_peer)

    acc_pre[...] = jnp.zeros_like(acc_pre)
    acc_act[...] = jnp.zeros_like(acc_act)

    def first_layer(c):
        ch = cols(c)
        await_bytes(xs.at[2, :, :, ch], agc_sem.at[c])
        await_bytes(xs.at[3, :, :, ch], agd_sem.at[c])
        acc_pre[...] += mm(xs[:, 0, :, ch].reshape(N_BLK * ROWS, CW), w1[ch, :])
        acc_act[...] += mm_nt(xs[:, 1, :, ch].reshape(N_BLK * ROWS, CW), w2[:, ch])

    def staged(step, stages):
        for lag, stage in stages:
            @pl.when((step >= lag) & (step < lag + NC))
            def _(stage=stage, lag=lag):
                stage(step - lag)

    loads[3].wait()
    loads[4].wait()

    @pl.loop(0, NC + 5)
    def _(step):
        staged(step, (
            (0, send_slots), (2, turn_slots), (3, gather_slots), (4, forward_slots),
            (5, first_layer),
        ))

    @pl.loop(0, 8)
    def _(b):
        rows = pl.ds(pl.multiple_of(b * 64, 64), 64)
        u = acc_pre[rows, :]
        square = u * u
        tangent = jnp.tanh(ROOT_TWO_OVER_PI * (u + CUBIC_TERM * square * u))
        hid[rows, :] = (0.5 * u * (1.0 + tangent)).astype(BF16)
        slope = 0.5 * (1.0 + tangent) + 0.5 * u * (1.0 - tangent * tangent) * ROOT_TWO_OVER_PI * (
            1.0 + 3.0 * CUBIC_TERM * square
        )
        pg[rows, :] = (acc_act[rows, :] * slope).astype(BF16)

    cg[...] = jnp.zeros_like(cg)
    dg[...] = jnp.zeros_like(dg)

    def second_layer(c):
        ch = cols(c)
        op[:, 0, :, ch] = mm(hid[...], w2[:, ch]).astype(BF16).reshape(N_BLK, ROWS, CW)
        op[:, 1, :, ch] = mm_nt(pg[...], w1[ch, :]).astype(BF16).reshape(N_BLK, ROWS, CW)
        remote(
            op.at[pl.ds(2, 2), :, :, ch], rc.at[:, :, :, ch], snd_sem.at[5], rc_sem.at[c], core_peer
        )

    def core_sum(c):
        ch = cols(c)
        await_bytes(rc.at[:, :, :, ch], rc_sem.at[c])
        sx[:, :, ch] = (op[1, :, :, ch].astype(F32) + rc[1, :, :, ch].astype(F32)).astype(BF16)
        remote(sx.at[:, :, ch], rx.at[:, :, ch], snd_sem.at[6], rx_sem.at[c], x_peer)
        t_own[:, :, ch] = op[0, :, :, ch].astype(F32) + rc[0, :, :, ch].astype(F32)

    def weight_grads(c):
        ch = cols(c)
        g1v[ch, :] = mm_tn(xs[:, 0, :, ch].reshape(N_BLK * ROWS, CW), pg[...]).astype(BF16)
        g2v[:, ch] = mm_tn(hid[...], xs[:, 1, :, ch].reshape(N_BLK * ROWS, CW)).astype(BF16)

    def x_sum(c):
        ch = cols(c)
        await_bytes(rx.at[:, :, ch], rx_sem.at[c])
        so[:, :, ch] = (t_own[:, :, ch] + rx[:, :, ch].astype(F32)).astype(BF16)
        mine = pl.ds(pl.multiple_of(yx * 16, 16), 16)
        pltpu.make_async_copy(so.at[:, mine, ch], ry.at[:, mine, ch], ry_sem.at[c]).start()

        @pl.loop(1, 8)
        def _(k):
            yxt, dev = yx_peer(k)
            remote(
                so.at[:, pl.ds(pl.multiple_of(yxt * 16, 16), 16), ch],
                ry.at[:, mine, ch], snd_sem.at[7], ry_sem.at[c], dev,
            )

    def turn_back(c):
        ch = cols(c)
        await_bytes(ry.at[:, :, ch], ry_sem.at[c])
        sz[:, ch] = mm_tn(perm1[...], ry[:, :, ch].reshape(2 * ROWS, CW)).astype(BF16)
        mine = pl.ds(pl.multiple_of(z * 32, 32), 32)
        pltpu.make_async_copy(sz.at[mine, ch], rz.at[mine, ch], rz_sem.at[c]).start()

        @pl.loop(1, 8)
        def _(k):
            zt, dev = z_peer(k)
            remote(
                sz.at[pl.ds(pl.multiple_of(zt * 32, 32), 32), ch], rz.at[mine, ch],
                snd_sem.at[8], rz_sem.at[c], dev,
            )

    def slots_back(c):
        ch = cols(c)
        await_bytes(rz.at[:, ch], rz_sem.at[c])
        rp[:, ch] = mm(perm3[...], rz[:, ch]).astype(BF16)
        for i in range(IMG):
            rows = pl.ds(i * TOK, TOK)
            cg[rows, :] += mm_nt(cot[rows, ch], rp[pl.ds(i * 128, EXP), ch])
            dg[rows, :] += mm_nt(tok[rows, ch], rp[pl.ds(i * 128 + EXP, EXP), ch])

    @pl.loop(0, NC + 6)
    def _(step):
        staged(step, (
            (0, second_layer), (1, core_sum), (1, weight_grads), (2, x_sum), (4, turn_back),
            (6, slots_back),
        ))

    stores = [
        pltpu.make_async_copy(g1v, g1_hbm, out_sem.at[0]),
        pltpu.make_async_copy(g2v, g2_hbm, out_sem.at[1]),
    ]
    for store in stores:
        store.start()

    for i in range(IMG):
        rows = pl.ds(i * TOK, TOK)
        d, c = disp[rows, :], comb[rows, :]
        d_grad, c_grad = dg[rows, :], cg[rows, :]
        grad = d * (d_grad - jnp.sum(d * d_grad, axis=0, keepdims=True))
        grad = grad + c * (c_grad - jnp.sum(c * c_grad, axis=1, keepdims=True))
        llow[rows, :] = grad.astype(BF16)

    e3, j3 = iota((EXP, EXP), 0), iota((EXP, EXP), 1)
    by_z = one_hot(e3 == (j3 & 7) * 8 + (j3 >> 3))
    turned = mm(llow[...], by_z).astype(BF16)
    part = mm_tn(turned, tok[...])
    for k in range(NZ):
        rows = part[k * 8:(k + 1) * 8]
        rsend[pl.ds(k * 16, 16), :] = jnp.concatenate(
            [rows[:, :HID], rows[:, HID:]], axis=0
        ).astype(BF16)
    mine_z = pl.ds(pl.multiple_of(z * 16, 16), 16)
    pltpu.make_async_copy(rsend.at[mine_z], rrecv.at[mine_z], rt_sem.at[0]).start()

    @pl.loop(1, 8)
    def _(k):
        zt, dev = z_peer(k)
        remote(
            rsend.at[pl.ds(pl.multiple_of(zt * 16, 16), 16)], rrecv.at[mine_z],
            snd_sem.at[9], rt_sem.at[0], dev,
        )

    for i in range(IMG):
        rows = pl.ds(i * TOK, TOK)

        @pl.loop(0, NC)
        def _(c, i=i, rows=rows):
            ch = cols(c)
            tgv[rows, ch] = (
                mm(dlow[rows, :], rp[pl.ds(i * 128 + EXP, EXP), ch]) + mm_nt(llow[rows, :], rt[ch, :])
            ).astype(BF16)

    stores.append(pltpu.make_async_copy(tgv, tg_hbm, out_sem.at[2]))
    stores[2].start()

    await_bytes(rrecv, rt_sem.at[0])
    total = rrecv[pl.ds(0, 16), :].astype(F32)
    for k in range(1, NZ):
        total = total + rrecv[pl.ds(k * 16, 16), :].astype(F32)
    for k in range(NYX):
        rs2[k, pl.ds(0, 1), :] = total[k:k + 1]
        rs2[k, pl.ds(1, 1), :] = total[8 + k:9 + k]
    pltpu.make_async_copy(rs2.at[yx], rr2.at[yx], rt_sem.at[1]).start()

    @pl.loop(1, 8)
    def _(k):
        yxt, dev = yx_peer(k)
        remote(rs2.at[yxt], rr2.at[yx], snd_sem.at[10], rt_sem.at[1], dev)

    await_bytes(rr2, rt_sem.at[1])
    rs3[...] = jnp.sum(rr2[...], axis=0)
    remote(rs3, rr3, snd_sem.at[11], rt_sem.at[2], x_peer)
    await_bytes(rr3, rt_sem.at[2])
    rs4[...] = rs3[...] + rr3[...]
    remote(rs4, rr4, snd_sem.at[12], rt_sem.at[3], core_peer)
    await_bytes(rr4, rt_sem.at[3])
    rg_out[...] = rs4[...] + rr4[...]

    for store in stores:
        store.wait()
    for ref, number in (
        (send1.at[pl.ds(0, 224)], 0), (send2.at[:, pl.ds(0, 112)], 1),
        (xs.at[0], 2), (xs.at[0], 3), (xs.at[1], 4), (rc, 5), (sx, 6),
        (so.at[:, pl.ds(0, 112)], 7), (sz.at[pl.ds(0, 224)], 8),
        (rsend.at[pl.ds(0, 112)], 9), (rs2.at[pl.ds(0, 7)], 10), (rs3, 11), (rs4, 12),
    ):
        await_bytes(ref, snd_sem.at[number])


def body(tokens, cotangent, router, first_weight, second_weight):
    vmem, dma = pltpu.VMEM, pltpu.SemaphoreType.DMA
    token_grad, router_column, first_grad, second_grad = pl.pallas_call(
        kernel,
        out_shape=(
            jax.ShapeDtypeStruct((IMG * TOK, DIM), BF16),
            jax.ShapeDtypeStruct((2, HID), F32),
            jax.ShapeDtypeStruct((DIM, HID), BF16),
            jax.ShapeDtypeStruct((HID, DIM), BF16),
        ),
        in_specs=[pl.BlockSpec(memory_space=pl.ANY)] * 5,
        out_specs=(
            pl.BlockSpec(memory_space=pl.ANY),
            pl.BlockSpec(memory_space=pltpu.VMEM),
            pl.BlockSpec(memory_space=pl.ANY),
            pl.BlockSpec(memory_space=pl.ANY),
        ),
        scratch_shapes=[
            vmem((IMG * TOK, DIM), BF16),
            vmem((IMG * TOK, DIM), BF16),
            vmem((DIM, EXP), BF16),
            vmem((DIM, HID), BF16),
            vmem((HID, DIM), BF16),
            vmem((256, 1024), BF16),
            vmem((IMG * TOK, EXP), F32),
            vmem((IMG * TOK, EXP), F32),
            vmem((IMG * TOK, EXP), BF16),
            vmem((256, 256), BF16),
            vmem((256, 256), BF16),
            vmem((256, DIM), BF16),
            vmem((256, DIM), BF16),
            vmem((2, ROWS, DIM), BF16),
            vmem((N_BLK, 2, ROWS, DIM), BF16),
            vmem((N_BLK * ROWS, HID), F32),
            vmem((N_BLK * ROWS, HID), F32),
            vmem((N_BLK * ROWS, HID), BF16),
            vmem((N_BLK * ROWS, HID), BF16),
            vmem((N_BLK, 2, ROWS, DIM), BF16),
            vmem((2, 2, ROWS, DIM), BF16),
            vmem((2, ROWS, DIM), F32),
            vmem((2, ROWS, DIM), BF16),
            vmem((2, ROWS, DIM), BF16),
            vmem((2, ROWS, DIM), BF16),
            vmem((2, ROWS, DIM), BF16),
            vmem((256, DIM), BF16),
            vmem((256, DIM), BF16),
            vmem((256, DIM), BF16),
            vmem((IMG * TOK, EXP), F32),
            vmem((IMG * TOK, EXP), F32),
            vmem((IMG * TOK, EXP), BF16),
            vmem((IMG * TOK, DIM), BF16),
            vmem((DIM, HID), BF16),
            vmem((HID, DIM), BF16),
            vmem((NZ * 16, HID), BF16),
            vmem((NZ * 16, HID), BF16),
            vmem((NYX, 2, HID), F32),
            vmem((NYX, 2, HID), F32),
            vmem((2, HID), F32),
            vmem((2, HID), F32),
            vmem((2, HID), F32),
            vmem((2, HID), F32),
            dma((5,)), dma((3,)),
            dma((NC,)), dma((NC,)), dma((NC,)), dma((NC,)), dma((NC,)),
            dma((NC,)), dma((NC,)), dma((NC,)), dma((NC,)),
            dma((4,)), dma((13,)),
        ],
        compiler_params=pltpu.CompilerParams(
            collective_id=0, has_side_effects=True, vmem_limit_bytes=56 * 1024 * 1024
        ),
    )(
        tokens.reshape(IMG * TOK, DIM), cotangent.reshape(IMG * TOK, DIM), router,
        first_weight[0], second_weight[0],
    )
    return (
        token_grad.reshape(IMG, TOK, DIM),
        router_column.reshape(DIM, 1),
        first_grad[None],
        second_grad[None],
    )


def solution(mesh):
    placed = (
        P(("dp", "expert"), None, None),
        P(("dp", "expert"), None, None),
        P(),
        P("expert", None, "dp"),
        P("expert", "dp", None),
    )
    return jax.shard_map(
        body,
        mesh=mesh,
        in_specs=placed,
        out_specs=(
            P(("dp", "expert"), None, None),
            P(None, "expert"),
            P("expert", None, "dp"),
            P("expert", "dp", None),
        ),
        check_vma=False,
    )
```

time: 230 us -> 97.8 us (0.43)
  Pallas kernels: 0 us -> 88.1 us
  waiting for transfers between devices: 84.3 us -> 0 us
  blocking collectives: 58.4 us -> 0 us
  matrix products: 32.9 us -> 0 us
  starting transfers between devices: 24.7 us -> 0 us
  between operations: 13.9 us -> 0.65 us
  other arithmetic: 3.75 us -> 0 us
  local copies, waits for them, and re-layouts: 11.4 us -> 8.87 us
    pallas_call x0 -> x1, Pallas kernels: none -> 88.1 us  [body(): pl.pallas_call(kernel, out_shape=(jax.ShapeDtypeStruct((IMG * TOK, DIM),...]
    all_to_all x2 -> x0, blocking collectives: 48.5 us -> none  [the longest x1 29.1 us: body(): lax.all_to_all(slot_in, 'expert', split_axis=1, concat_axis=0, tiled=True)]
    reduce_scatter x1 -> x0, waiting for transfers between devices: 36 us -> none  [body(): lax.psum_scatter(jnp.concatenate([forward_part, backward_part], axis=1).a...]
    dot_general x14 -> x0, matrix products: 32.9 us -> none  [the longest x2 7.7 us: matmul_tn(): lax.dot_general(left, right, (((0,), (0,)), ((), ())), preferred_element_...]
    all_to_all x3 -> x0, starting transfers between devices: 24.6 us -> none  [the longest x1 12.3 us: body(): lax.all_to_all(shaped_back, 'expert', split_axis=0, concat_axis=2, tiled=...]
    all_gather x2 -> x0, waiting for transfers between devices: 24.1 us -> none  [the longest x1 22.4 us: body(): lax.all_gather(mine_grad, 'dp', axis=0, tiled=True)]
    all_to_all x3 -> x0, waiting for transfers between devices: 24.1 us -> none  [the longest x1 12.8 us: body(): lax.all_to_all(shaped_back, 'expert', split_axis=0, concat_axis=2, tiled=...]
    psum x1 -> x0, blocking collectives: 9.93 us -> none  [body(): router_grad = lax.psum(jnp.sum(router_parts, axis=0), 'dp')[:, None]]
  transfers between devices with their start and end apart: 6 -> 0, of which waited for: 6 -> 0; matrix products, arithmetic and copies ran while one was open for 11% -> 0% of each run, Pallas kernels for 0% -> 0%
where the time goes in v2:
time: 97.8 us; the launch traced here: 97.6 us
  Pallas kernels  88.1 us (90%)
  local copies, waits for them, and re-layouts  8.87 us (9%)
    pallas_call x1, Pallas kernels, body(): pl.pallas_call(kernel, out_shape=(jax.ShapeDtypeStruct((IMG * TOK, DIM),...  88.1 us
    unnamed x9, local copies, waits for them, and re-layouts  8.87 us

profile of v2, /device:TPU:1, one launch (start us, length us, event | category | flops | bytes accessed | tf_op | source)
XLA Modules:
  0.0 97.6 jit_solution(7064059111209324891)
XLA Ops:
  0.6 1.8 %copy.9.rt_hbm = bf16[1280,64]{1,0:T(8,128)(2,1)} copy(bf16[1280,64]{0,1:T(8,128)(2,1)} %param.7) | data formatting | bytes 327680 | tf_op args[2]
  2.4 88.1 %shard_map.84 = (bf16[512,1280]{1,0:T(8,128)(2,1)}, f32[2,640]{1,0:T(2,128)}, bf16[1280,640]{1,0:T(8,128)(2,1)}, bf16[640,1280]{1,0:T(8,128)(2,1)}) custom-call(bf16[512,1280]{1,0:T(8,128)(2,1)} %bitcast.16, bf16[512,1280]{1,0:T(8,128)(2,1)} %bitcast.17, bf16[1280,64]{1,0:T(8,128)(2,1)} %copy.9.rt_hbm, bf16[1280,640]{1,0:T(8,128)(2,1)} %bitcast.11, ...), custom_call_target="tpu_custom_call" | custom-call | tf_op jit(solution)/shard_map/pallas_call | solution.py:369
  90.5 0.0 copy-start.1
  90.6 1.4 %copy.10 = f32[1,1,2,640]{3,1,2,0:T(1,128)} copy(f32[1,1,2,640]{3,2,1,0:T(2,128)} %bitcast.19) | data formatting | bytes 10240
  92.0 2.5 %copy.14 = bf16[2,256,1280]{2,1,0:T(8,128)(2,1)} copy(bf16[2,256,1280]{2,1,0:T(8,128)(2,1)} %bitcast.15) | data formatting | bytes 2621440
  94.4 0.0 copy-done.1
  94.4 0.0 copy-start
  94.4 1.2 %copy.15 = bf16[1,1280,640]{2,1,0:T(8,128)(2,1)} copy(bf16[1,1280,640]{2,1,0:T(8,128)(2,1)S(1)} %bitcast.14) | data formatting | bytes 3276800
  95.6 0.9 copy-done
  96.5 1.2 %copy.16 = bf16[1,640,1280]{2,1,0:T(8,128)(2,1)} copy(bf16[1,640,1280]{2,1,0:T(8,128)(2,1)S(1)} %bitcast.13) | data formatting | bytes 3276800
Async XLA Ops:
  90.5 3.9 %copy-start.1 = (bf16[1280,640]{1,0:T(8,128)(2,1)S(1)}, bf16[1280,640]{1,0:T(8,128)(2,1)}, u32[]{:S(2)}) copy-start(bf16[1280,640]{1,0:T(8,128)(2,1)} %get-tuple-element.10) | copy-start | bytes 4915204
  94.4 2.0 %copy-start = (bf16[640,1280]{1,0:T(8,128)(2,1)S(1)}, bf16[640,1280]{1,0:T(8,128)(2,1)}, u32[]{:S(2)}) copy-start(bf16[640,1280]{1,0:T(8,128)(2,1)} %get-tuple-element.11) | copy-start | bytes 4915204

commit v3 on v2

--- a/solution.py
+++ b/solution.py
@@ -42,12 +42,12 @@
 
 def kernel(
     tok_hbm, cot_hbm, rt_hbm, w1_hbm, w2_hbm,
-    tg_hbm, rg_out, g1_hbm, g2_hbm,
+    tgv, rg_out, g1v, g2v,
     tok, cot, rt, w1, w2, ltm, disp, comb, dlow, perm1, perm3,
     send1, recv1, send2, xs, acc_pre, acc_act, hid, pg,
     op, rc, t_own, sx, rx, so, ry, sz, rz, rp, cg, dg, llow,
-    tgv, g1v, g2v, rsend, rrecv, rs2, rr2, rs3, rr3, rs4, rr4,
-    in_sem, out_sem, z1_sem, y1_sem, agx_sem, agc_sem, agd_sem,
+    rsend, rrecv, rs2, rr2, rs3, rr3,
+    in_sem, z1_sem, y1_sem, agx_sem, agc_sem, agd_sem,
     rc_sem, rx_sem, ry_sem, rz_sem, rt_sem, snd_sem,
 ):
     p = lax.axis_index("dp")
@@ -58,7 +58,7 @@
     xh = yx % 2
 
     def z_peer(k):
-        zt = (z + k) % NZ
+        zt = (z + (k + 1) // 2 * (2 * (k % 2) - 1) + NZ) % NZ
         return zt, (p, yx * NZ + zt)
 
     def yx_peer(k):
@@ -98,8 +98,8 @@
         pl.semaphore_signal(barrier, inc=1, device_id=z_peer(k)[1], device_id_type=MESH)
         pl.semaphore_signal(barrier, inc=1, device_id=yx_peer(k)[1], device_id_type=MESH)
 
-    pl.semaphore_signal(barrier, inc=1, device_id=core_peer, device_id_type=MESH)
-    pl.semaphore_signal(barrier, inc=1, device_id=x_peer, device_id_type=MESH)
+    for k in range(1, 4):
+        pl.semaphore_signal(barrier, inc=1, device_id=((p + k) % 4, q), device_id_type=MESH)
 
     o1, n1 = iota((256, 256), 0), iota((256, 256), 1)
     perm1[...] = one_hot(
@@ -113,7 +113,7 @@
 
     loads[0].wait()
     loads[1].wait()
-    logits = mm(tok[...], rt[...])
+    logits = mm_nt(tok[...], rt[...])
     for i in range(IMG):
         rows = pl.ds(i * TOK, TOK)
         part = logits[i * TOK:(i + 1) * TOK]
@@ -129,7 +129,7 @@
             spread = one_hot(same_slot & ((n2 & 3) == a * 2 + i))
             ltm[:, pl.ds(a * 512 + i * TOK, TOK)] = mm_nt(spread, low).astype(BF16)
     loads[2].wait()
-    pl.semaphore_wait(barrier, 16)
+    pl.semaphore_wait(barrier, 17)
 
     def send_slots(c):
         ch = cols(c)
@@ -282,13 +282,6 @@
             (6, slots_back),
         ))
 
-    stores = [
-        pltpu.make_async_copy(g1v, g1_hbm, out_sem.at[0]),
-        pltpu.make_async_copy(g2v, g2_hbm, out_sem.at[1]),
-    ]
-    for store in stores:
-        store.start()
-
     for i in range(IMG):
         rows = pl.ds(i * TOK, TOK)
         d, c = disp[rows, :], comb[rows, :]
@@ -324,11 +317,8 @@
         def _(c, i=i, rows=rows):
             ch = cols(c)
             tgv[rows, ch] = (
-                mm(dlow[rows, :], rp[pl.ds(i * 128 + EXP, EXP), ch]) + mm_nt(llow[rows, :], rt[ch, :])
+                mm(dlow[rows, :], rp[pl.ds(i * 128 + EXP, EXP), ch]) + mm(llow[rows, :], rt[:, ch])
             ).astype(BF16)
-
-    stores.append(pltpu.make_async_copy(tgv, tg_hbm, out_sem.at[2]))
-    stores[2].start()
 
     await_bytes(rrecv, rt_sem.at[0])
     total = rrecv[pl.ds(0, 16), :].astype(F32)
@@ -346,45 +336,50 @@
 
     await_bytes(rr2, rt_sem.at[1])
     rs3[...] = jnp.sum(rr2[...], axis=0)
-    remote(rs3, rr3, snd_sem.at[11], rt_sem.at[2], x_peer)
+    pltpu.make_async_copy(rs3, rr3.at[p], rt_sem.at[2]).start()
+    for k in range(1, 4):
+        remote(rs3, rr3.at[p], snd_sem.at[11], rt_sem.at[2], ((p + k) % 4, q))
     await_bytes(rr3, rt_sem.at[2])
-    rs4[...] = rs3[...] + rr3[...]
-    remote(rs4, rr4, snd_sem.at[12], rt_sem.at[3], core_peer)
-    await_bytes(rr4, rt_sem.at[3])
-    rg_out[...] = rs4[...] + rr4[...]
-
-    for store in stores:
-        store.wait()
+    rg_out[...] = (rr3[0] + rr3[1]) + (rr3[2] + rr3[3])
+
     for ref, number in (
         (send1.at[pl.ds(0, 224)], 0), (send2.at[:, pl.ds(0, 112)], 1),
         (xs.at[0], 2), (xs.at[0], 3), (xs.at[1], 4), (rc, 5), (sx, 6),
         (so.at[:, pl.ds(0, 112)], 7), (sz.at[pl.ds(0, 224)], 8),
-        (rsend.at[pl.ds(0, 112)], 9), (rs2.at[pl.ds(0, 7)], 10), (rs3, 11), (rs4, 12),
+        (rsend.at[pl.ds(0, 112)], 9), (rs2.at[pl.ds(0, 7)], 10), (rr3.at[pl.ds(0, 3)], 11),
     ):
         await_bytes(ref, snd_sem.at[number])
 
 
+def store_kernel(tg, rg, g1, g2, tg_hbm, rg_out, g1_hbm, g2_hbm, sem):
+    stores = [
+        pltpu.make_async_copy(a, b, sem.at[i])
+        for i, (a, b) in enumerate(((g1, g1_hbm), (g2, g2_hbm), (tg, tg_hbm)))
+    ]
+    for store in stores:
+        store.start()
+    rg_out[:, :HID] = rg[0:1, :]
+    rg_out[:, HID:] = rg[1:2, :]
+    for store in stores:
+        store.wait()
+
+
 def body(tokens, cotangent, router, first_weight, second_weight):
     vmem, dma = pltpu.VMEM, pltpu.SemaphoreType.DMA
-    token_grad, router_column, first_grad, second_grad = pl.pallas_call(
+    results = pl.pallas_call(
         kernel,
         out_shape=(
-            jax.ShapeDtypeStruct((IMG * TOK, DIM), BF16),
-            jax.ShapeDtypeStruct((2, HID), F32),
-            jax.ShapeDtypeStruct((DIM, HID), BF16),
-            jax.ShapeDtypeStruct((HID, DIM), BF16),
+            vmem((IMG * TOK, DIM), BF16),
+            vmem((2, HID), F32),
+            vmem((DIM, HID), BF16),
+            vmem((HID, DIM), BF16),
         ),
-        in_specs=[pl.BlockSpec(memory_space=pl.ANY)] * 5,
-        out_specs=(
-            pl.BlockSpec(memory_space=pl.ANY),
-            pl.BlockSpec(memory_space=pltpu.VMEM),
-            pl.BlockSpec(memory_space=pl.ANY),
-            pl.BlockSpec(memory_space=pl.ANY),
-        ),
+        in_specs=[pl.BlockSpec(memory_space=pltpu.HBM)] * 5,
+        out_specs=(pl.BlockSpec(memory_space=pltpu.VMEM),) * 4,
         scratch_shapes=[
             vmem((IMG * TOK, DIM), BF16),
             vmem((IMG * TOK, DIM), BF16),
-            vmem((DIM, EXP), BF16),
+            vmem((EXP, DIM), BF16),
             vmem((DIM, HID), BF16),
             vmem((HID, DIM), BF16),
             vmem((256, 1024), BF16),
@@ -414,29 +409,42 @@
             vmem((IMG * TOK, EXP), F32),
             vmem((IMG * TOK, EXP), F32),
             vmem((IMG * TOK, EXP), BF16),
-            vmem((IMG * TOK, DIM), BF16),
-            vmem((DIM, HID), BF16),
-            vmem((HID, DIM), BF16),
             vmem((NZ * 16, HID), BF16),
             vmem((NZ * 16, HID), BF16),
             vmem((NYX, 2, HID), F32),
             vmem((NYX, 2, HID), F32),
             vmem((2, HID), F32),
-            vmem((2, HID), F32),
-            vmem((2, HID), F32),
-            vmem((2, HID), F32),
-            dma((5,)), dma((3,)),
+            vmem((4, 2, HID), F32),
+            dma((5,)),
             dma((NC,)), dma((NC,)), dma((NC,)), dma((NC,)), dma((NC,)),
             dma((NC,)), dma((NC,)), dma((NC,)), dma((NC,)),
-            dma((4,)), dma((13,)),
+            dma((3,)), dma((12,)),
         ],
         compiler_params=pltpu.CompilerParams(
             collective_id=0, has_side_effects=True, vmem_limit_bytes=56 * 1024 * 1024
         ),
     )(
-        tokens.reshape(IMG * TOK, DIM), cotangent.reshape(IMG * TOK, DIM), router,
+        tokens.reshape(IMG * TOK, DIM), cotangent.reshape(IMG * TOK, DIM), router.T,
         first_weight[0], second_weight[0],
     )
+    token_grad, router_column, first_grad, second_grad = pl.pallas_call(
+        store_kernel,
+        out_shape=(
+            jax.ShapeDtypeStruct((IMG * TOK, DIM), BF16),
+            jax.ShapeDtypeStruct((1, DIM), F32),
+            jax.ShapeDtypeStruct((DIM, HID), BF16),
+            jax.ShapeDtypeStruct((HID, DIM), BF16),
+        ),
+        in_specs=[pl.BlockSpec(memory_space=pltpu.VMEM)] * 4,
+        out_specs=(
+            pl.BlockSpec(memory_space=pl.ANY),
+            pl.BlockSpec(memory_space=pltpu.VMEM),
+            pl.BlockSpec(memory_space=pl.ANY),
+            pl.BlockSpec(memory_space=pl.ANY),
+        ),
+        scratch_shapes=[dma((3,))],
+        compiler_params=pltpu.CompilerParams(vmem_limit_bytes=8 * 1024 * 1024),
+    )(*results)
     return (
         token_grad.reshape(IMG, TOK, DIM),
         router_column.reshape(DIM, 1),

time: 97.8 us -> 92.9 us (0.950)
  local copies, waits for them, and re-layouts: 8.87 us -> 0 us
  Pallas kernels: 88.1 us -> 92.2 us
    unnamed x9 -> x0, local copies, waits for them, and re-layouts: 8.87 us -> none
    pallas_call x1 -> x2, Pallas kernels: 88.1 us -> 92.2 us  [the longest x1 89.5 us: body(): pl.pallas_call(kernel, out_shape=(vmem((IMG * TOK, DIM), BF16), vmem((2,...]
where the time goes in v3:
time: 92.9 us
  Pallas kernels  92.2 us (99%)
    pallas_call x1, Pallas kernels, body(): pl.pallas_call(kernel, out_shape=(vmem((IMG * TOK, DIM), BF16), vmem((2,...  89.5 us
    pallas_call x1, Pallas kernels, body(): pl.pallas_call(store_kernel, out_shape=(jax.ShapeDtypeStruct((IMG * TOK,...  2.76 us

profile of v3, /device:TPU:1, one launch (start us, length us, event | category | flops | bytes accessed | tf_op | source)
XLA Modules:
  0.0 92.9 jit_solution(2370527976810962984)
XLA Ops:
  0.6 89.5 %shard_map.84 = (bf16[512,1280]{1,0:T(8,128)(2,1)S(1)}, f32[2,640]{1,0:T(2,128)S(1)}, bf16[1280,640]{1,0:T(8,128)(2,1)S(1)}, bf16[640,1280]{1,0:T(8,128)(2,1)S(1)}) custom-call(bf16[512,1280]{1,0:T(8,128)(2,1)} %bitcast.11, bf16[512,1280]{1,0:T(8,128)(2,1)} %bitcast.12, bf16[64,1280]{1,0:T(8,128)(2,1)} %bitcast.13, bf16[1280,640]{1,0:T(8,128)(2,1)} %bitcast.9, ...), custom_call_target="tpu_custom_call" | custom-call | tf_op jit(solution)/shard_map/pallas_call | solution.py:369
  90.1 2.8 %shard_map.85 = (bf16[512,1280]{1,0:T(8,128)(2,1)}, f32[1,1280]{1,0:T(1,128)}, bf16[1280,640]{1,0:T(8,128)(2,1)}, bf16[640,1280]{1,0:T(8,128)(2,1)}) custom-call(bf16[512,1280]{1,0:T(8,128)(2,1)S(1)} %get-tuple-element.12.tg, f32[2,640]{1,0:T(2,128)S(1)} %get-tuple-element.13.rg, bf16[1280,640]{1,0:T(8,128)(2,1)S(1)} %get-tuple-element.14.g1, ...), custom_call_target="tpu_custom_call" | custom-call | tf_op jit(solution)/shard_map/pallas_call | solution.py:430

commit v4 on v3

v4 whole, which is shorter than its diff:
```python
import functools

import jax
import jax.numpy as jnp
from jax import lax
from jax.experimental import pallas as pl
from jax.experimental.pallas import tpu as pltpu
from jax.sharding import PartitionSpec as P

ROOT_TWO_OVER_PI = 0.7978845608028654
CUBIC_TERM = 0.044715
MESH = pl.DeviceIdType.MESH
F32, BF16 = jnp.float32, jnp.bfloat16

NZ, NYX = 8, 8
IMG, TOK, DIM, HID, EXP = 2, 256, 1280, 640, 64
CW = 256
NC = DIM // CW
N_BLK = 4
UNITS = 2 * NC
LAST = 38


def mm(a, b):
    return lax.dot_general(a, b, (((1,), (0,)), ((), ())), preferred_element_type=F32)


def mm_nt(a, b):
    return lax.dot_general(a, b, (((1,), (1,)), ((), ())), preferred_element_type=F32)


def mm_tn(a, b):
    return lax.dot_general(a, b, (((0,), (0,)), ((), ())), preferred_element_type=F32)


def iota(shape, axis):
    return lax.broadcasted_iota(jnp.int32, shape, axis)


def one_hot(mask):
    return jnp.where(mask, 1.0, 0.0).astype(BF16)


def kernel(
    tok_hbm, cot_hbm, rt_hbm, w1_hbm, w2_hbm,
    tgv, rg_out, g1v, g2v,
    tok, cot, rt, rtj, w1, w2, ltm, disp, comb, dlow, perm1, perm3,
    send1, recv1, send2, xs, acc_pre, acc_act, hid, pg,
    op, rc, t_own, sx, rx, so, ry, sz, rz, rp, cgx, dgx, low2,
    rsend, rrecv, rs2, rr2, rs3, rr3,
    in_sem, z1_sem, y1_sem, agx_sem, agc_sem, agd_sem,
    rc_sem, rx_sem, ry_sem, rz_sem, rt_sem, snd_sem,
):
    p = lax.axis_index("dp")
    q = lax.axis_index("expert")
    z = lax.rem(q, NZ)
    yx = lax.div(q, NZ)
    y = lax.div(yx, 2)
    xh = lax.rem(yx, 2)

    z_at = [lax.rem(z + far, NZ) for far in (1, 7, 2, 6, 3, 5, 4)]
    z_peers = [(zt, (p, yx * NZ + zt)) for zt in z_at]
    p_flip = lax.rem(p + 2, 4)
    p_at, xh_at = (p, p_flip), (xh, 1 - xh)

    def yx_peer(dy, dx):
        yxt = lax.rem(y + dy, 4) * 2 + xh_at[dx]
        return yxt, (p_at[dx], yxt * NZ + z)

    yx_peers = [yx_peer(k // 2, k % 2) for k in range(1, 8)]
    core_peer = (p + 1 - 2 * lax.rem(p, 2), q)
    x_peer = (p_flip, q)
    dp_peers = [(lax.rem(p + k, 4), q) for k in range(1, 4)]

    def remote(src, dst, send_sem, recv_sem, dev):
        pltpu.make_async_remote_copy(
            src_ref=src, dst_ref=dst, send_sem=send_sem, recv_sem=recv_sem,
            device_id=dev, device_id_type=MESH,
        ).start()

    def await_bytes(ref, sem):
        pltpu.make_async_copy(ref, ref, sem).wait()

    def split(u):
        c = lax.rem(u, NC)
        return lax.div(u, NC), c, pl.ds(pl.multiple_of(c * CW, CW), CW)

    def rows_at(index, size):
        return pl.ds(pl.multiple_of(index * size, size), size)

    loads = [
        pltpu.make_async_copy(a, b, in_sem.at[i])
        for i, (a, b) in enumerate(
            ((rt_hbm, rt), (tok_hbm, tok), (cot_hbm, cot), (w1_hbm, w1), (w2_hbm, w2))
        )
    ]
    for load in loads[:3]:
        load.start()

    barrier = pltpu.get_barrier_semaphore()

    for dev in [dev for _, dev in z_peers + yx_peers] + dp_peers:
        pl.semaphore_signal(barrier, inc=1, device_id=dev, device_id_type=MESH)

    o1, n1 = iota((128, 128), 0), iota((128, 128), 1)
    perm1[...] = one_hot(
        n1 == ((o1 >> 1) & 7) * 16 + ((o1 >> 4) & 3) * 4 + (o1 >> 6) * 2 + (o1 & 1)
    )
    perm3[...] = one_hot(n1 == (o1 & 31) * 4 + ((o1 >> 5) & 1) * 2 + (o1 >> 6))

    def expert_of(j):
        y_at = (y + (j >> 5) * 2 + ((j >> 1) & 1)) & 3
        return (y_at * 2 + ((xh + j) & 1)) * 8 + ((j >> 2) & 7)

    n2, j2 = iota((256, EXP), 0), iota((256, EXP), 1)
    same_slot = j2 == n2 >> 2

    loads[0].wait()
    by_slot = one_hot(iota((EXP, EXP), 1) == expert_of(iota((EXP, EXP), 0)))
    rtj[...] = mm(by_slot, rt[...]).astype(BF16)
    loads[1].wait()
    loads[3].start()
    loads[4].start()
    logits = mm_nt(tok[...], rtj[...])
    for i in range(IMG):
        rows = pl.ds(i * TOK, TOK)
        part = logits[i * TOK:(i + 1) * TOK]
        up = jnp.exp(part - jnp.max(part, axis=0, keepdims=True))
        d = up / jnp.sum(up, axis=0, keepdims=True)
        up = jnp.exp(part - jnp.max(part, axis=1, keepdims=True))
        c = up / jnp.sum(up, axis=1, keepdims=True)
        disp[rows, :] = d
        comb[rows, :] = c
        d_low = d.astype(BF16)
        dlow[rows, :] = d_low
        for a, low in ((0, d_low), (1, c.astype(BF16))):
            spread = one_hot(same_slot & ((n2 & 3) == a * 2 + i))
            ltm[:, pl.ds(a * 512 + i * TOK, TOK)] = mm_nt(spread, low).astype(BF16)
    loads[2].wait()
    pl.semaphore_wait(barrier, 17)

    def send_slots(u):
        h, c, ch = split(u)
        rows = rows_at(h, 128)
        send1[u] = (
            mm(ltm[rows, :512], tok[:, ch]) + mm(ltm[rows, 512:], cot[:, ch])
        ).astype(BF16)
        mine = rows_at(z, 16)
        recv1[u, mine] = send1[u, mine]

        for zt, dev in z_peers:
            remote(
                send1.at[u, rows_at(zt, 16)], recv1.at[u, mine],
                snd_sem.at[0], z1_sem.at[u], dev,
            )

    def to_neighbours(h, src, dst, send_sem, recv_sem, sign):
        @pl.when(h == 0)
        def _():
            pltpu.make_async_copy(src(0), dst(0), recv_sem).start()

        @pl.when(h == 1)
        def _():
            remote(src(0), dst(0), send_sem, recv_sem, yx_peer(2, 0)[1])

        start = 2 * h if sign > 0 else 8 - 2 * h
        for k in range(1, 4):
            remote(src(k), dst(k), send_sem, recv_sem, yx_peer(start + sign * (k // 2), k % 2)[1])

    def turn_slots(u):
        h, c, ch = split(u)
        await_bytes(recv1.at[u, pl.ds(0, 112)], z1_sem.at[u])
        send2[u] = mm(perm1[...], recv1[u]).astype(BF16).reshape(2, 64, CW)
        to_neighbours(
            h, lambda k: send2.at[u, :, rows_at(k, 16)],
            lambda k: xs.at[u, 0, :, rows_at(k, 16)], snd_sem.at[1], y1_sem.at[u], 1,
        )

    def gather_slots(u):
        h, c, ch = split(u)
        await_bytes(xs.at[u, 0], y1_sem.at[u])
        remote(xs.at[u, 0], xs.at[u, 1], snd_sem.at[2], agx_sem.at[u], x_peer)
        remote(xs.at[u, 0], xs.at[u, 2], snd_sem.at[3], agc_sem.at[u], core_peer)

    def forward_slots(u):
        h, c, ch = split(u)
        await_bytes(xs.at[u, 1], agx_sem.at[u])
        remote(xs.at[u, 1], xs.at[u, 3], snd_sem.at[4], agd_sem.at[u], core_peer)

    def first_layer(u):
        h, c, ch = split(u)
        await_bytes(xs.at[u, 2], agc_sem.at[u])
        await_bytes(xs.at[u, 3], agd_sem.at[u])
        acc_pre[h] += mm(xs[u, :, 0].reshape(256, CW), w1[ch, :])
        acc_act[h] += mm_nt(xs[u, :, 1].reshape(256, CW), w2[:, ch])

        @pl.when(c == NC - 1)
        def _():
            @pl.loop(0, 4)
            def _(b):
                rows = rows_at(b, 64)
                v = acc_pre[h, rows, :]
                square = v * v
                tangent = jnp.tanh(ROOT_TWO_OVER_PI * (v + CUBIC_TERM * square * v))
                hid[h, rows, :] = (0.5 * v * (1.0 + tangent)).astype(BF16)
                slope = 0.5 * (1.0 + tangent) + 0.5 * v * (
                    1.0 - tangent * tangent
                ) * ROOT_TWO_OVER_PI * (1.0 + 3.0 * CUBIC_TERM * square)
                pg[h, rows, :] = (acc_act[h, rows, :] * slope).astype(BF16)

    def second_layer(u):
        h, c, ch = split(u)
        op[u, :, 0] = mm(hid[h], w2[:, ch]).astype(BF16).reshape(N_BLK, 64, CW)
        op[u, :, 1] = mm_nt(pg[h], w1[ch, :]).astype(BF16).reshape(N_BLK, 64, CW)
        remote(
            op.at[u, pl.ds(2, 2)], rc.at[u],
            snd_sem.at[5], rc_sem.at[u], core_peer,
        )

    def core_sum(u):
        h, c, ch = split(u)
        await_bytes(rc.at[u], rc_sem.at[u])
        sx[u] = (
            op[u, 1].astype(F32) + rc[u, 1].astype(F32)
        ).astype(BF16)
        remote(sx.at[u], rx.at[u], snd_sem.at[6], rx_sem.at[u], x_peer)
        t_own[u] = op[u, 0].astype(F32) + rc[u, 0].astype(F32)

    def weight_grads(c):
        ch = pl.ds(pl.multiple_of(c * CW, CW), CW)
        g1v[ch, :] = (
            mm_tn(xs[c, :, 0].reshape(256, CW), pg[0])
            + mm_tn(xs[NC + c, :, 0].reshape(256, CW), pg[1])
        ).astype(BF16)
        g2v[:, ch] = (
            mm_tn(hid[0], xs[c, :, 1].reshape(256, CW))
            + mm_tn(hid[1], xs[NC + c, :, 1].reshape(256, CW))
        ).astype(BF16)

    def x_sum(u):
        h, c, ch = split(u)
        await_bytes(rx.at[u], rx_sem.at[u])
        so[u] = (t_own[u] + rx[u].astype(F32)).astype(BF16)
        to_neighbours(
            h, lambda k: so.at[u, :, rows_at(k, 16)],
            lambda k: ry.at[u, :, rows_at(k, 16)], snd_sem.at[7], ry_sem.at[u], -1,
        )

    def turn_back(u):
        h, c, ch = split(u)
        await_bytes(ry.at[u], ry_sem.at[u])
        sz[u] = mm_tn(perm1[...], ry[u].reshape(128, CW)).astype(BF16)
        mine = rows_at(z, 16)
        rz[u, mine] = sz[u, mine]

        for zt, dev in z_peers:
            remote(
                sz.at[u, rows_at(zt, 16)], rz.at[u, mine],
                snd_sem.at[8], rz_sem.at[u], dev,
            )

    def slots_back(u):
        h, c, ch = split(u)
        await_bytes(rz.at[u, pl.ds(0, 112)], rz_sem.at[u])
        rp[h, :, ch] = mm(perm3[...], rz[u]).astype(BF16)
        for i in range(IMG):
            rows = pl.ds(i * TOK, TOK)
            slots = rp[h, pl.ds(i * 64, 64), ch]
            cgx[h, rows, :] += mm_nt(cot[rows, ch], slots)
            dgx[h, rows, :] += mm_nt(tok[rows, ch], slots)

    @pl.loop(0, LAST)
    def _(step):
        for lag, count, stage in (
            (0, UNITS, send_slots), (16, UNITS, second_layer), (23, UNITS, turn_back),
            (7, UNITS, gather_slots), (20, UNITS, x_sum), (31, NC, weight_grads),
            (4, UNITS, turn_slots), (28, UNITS, slots_back), (10, UNITS, forward_slots),
            (17, UNITS, core_sum), (11, UNITS, first_layer),
        ):
            @pl.when((step >= lag) & (step < lag + count))
            def _(stage=stage, lag=lag):
                stage(step - lag)

        @pl.when(step == 0)
        def _():
            for ref in (acc_pre, acc_act, cgx, dgx):
                ref[...] = jnp.zeros_like(ref)
            loads[3].wait()
            loads[4].wait()

    c_grads = jnp.concatenate([cgx[0, :, :32], cgx[1, :, :32]], axis=1)
    d_grads = jnp.concatenate([dgx[0, :, 32:], dgx[1, :, 32:]], axis=1)
    for i in range(IMG):
        rows = pl.ds(i * TOK, TOK)
        d, c = disp[rows, :], comb[rows, :]
        d_grad, c_grad = d_grads[i * TOK:(i + 1) * TOK], c_grads[i * TOK:(i + 1) * TOK]
        grad = d * (d_grad - jnp.sum(d * d_grad, axis=0, keepdims=True))
        grad = grad + c * (c_grad - jnp.sum(c * c_grad, axis=1, keepdims=True))
        low2[rows, :64] = dlow[rows, :]
        low2[rows, 64:] = grad.astype(BF16)

    e3, j3 = iota((EXP, EXP), 1), iota((EXP, EXP), 0)
    by_z = one_hot(expert_of(j3) == (e3 & 7) * 8 + (e3 >> 3))
    turned = mm(low2[:, 64:], by_z).astype(BF16)
    part = mm_tn(turned, tok[...])
    for k in range(NZ):
        rows = part[k * 8:(k + 1) * 8]
        rsend[pl.ds(k * 16, 16), :] = jnp.concatenate(
            [rows[:, :HID], rows[:, HID:]], axis=0
        ).astype(BF16)
    mine_z = rows_at(z, 16)
    pltpu.make_async_copy(rsend.at[mine_z], rrecv.at[mine_z], rt_sem.at[0]).start()

    for zt, dev in z_peers:
        remote(rsend.at[rows_at(zt, 16)], rrecv.at[mine_z], snd_sem.at[9], rt_sem.at[0], dev)

    for i in range(IMG):
        rows = pl.ds(i * TOK, TOK)

        @pl.loop(0, NC)
        def _(c, i=i, rows=rows):
            ch = pl.ds(pl.multiple_of(c * CW, CW), CW)
            back = pl.ds(i * 64 + 32, 32)
            right = jnp.concatenate([rp[0, back, ch], rp[1, back, ch], rtj[:, ch]], axis=0)
            tgv[rows, ch] = mm(low2[rows, :], right).astype(BF16)

    await_bytes(rrecv, rt_sem.at[0])
    total = rrecv[pl.ds(0, 16), :].astype(F32)
    for k in range(1, NZ):
        total = total + rrecv[pl.ds(k * 16, 16), :].astype(F32)
    for k in range(NYX):
        rs2[k, pl.ds(0, 1), :] = total[k:k + 1]
        rs2[k, pl.ds(1, 1), :] = total[8 + k:9 + k]
    pltpu.make_async_copy(rs2.at[yx], rr2.at[yx], rt_sem.at[1]).start()

    for yxt, dev in yx_peers:
        remote(rs2.at[yxt], rr2.at[yx], snd_sem.at[10], rt_sem.at[1], dev)

    await_bytes(rr2, rt_sem.at[1])
    rs3[...] = jnp.sum(rr2[...], axis=0)
    pltpu.make_async_copy(rs3, rr3.at[p], rt_sem.at[2]).start()
    for dev in dp_peers:
        remote(rs3, rr3.at[p], snd_sem.at[11], rt_sem.at[2], dev)
    await_bytes(rr3, rt_sem.at[2])
    rg_out[...] = (rr3[0] + rr3[1]) + (rr3[2] + rr3[3])

    seven = send1.at[:, pl.ds(0, 112)]
    for ref, number in (
        (seven, 0), (seven, 1), (xs.at[:, 0], 2), (xs.at[:, 0], 3), (xs.at[:, 1], 4),
        (rc, 5), (sx, 6), (seven, 7), (seven, 8),
        (rsend.at[pl.ds(0, 112)], 9), (rs2.at[pl.ds(0, 7)], 10), (rr3.at[pl.ds(0, 3)], 11),
    ):
        await_bytes(ref, snd_sem.at[number])


def store_kernel(tg, rg, g1, g2, tg_hbm, rg_out, g1_hbm, g2_hbm, sem):
    stores = [
        pltpu.make_async_copy(a, b, sem.at[i])
        for i, (a, b) in enumerate(((g1, g1_hbm), (g2, g2_hbm), (tg, tg_hbm)))
    ]
    for store in stores:
        store.start()
    rg_out[:, :HID] = rg[0:1, :]
    rg_out[:, HID:] = rg[1:2, :]
    for store in stores:
        store.wait()


def body(tokens, cotangent, router, first_weight, second_weight):
    vmem, dma = pltpu.VMEM, pltpu.SemaphoreType.DMA
    results = pl.pallas_call(
        kernel,
        out_shape=(
            vmem((IMG * TOK, DIM), BF16),
            vmem((2, HID), F32),
            vmem((DIM, HID), BF16),
            vmem((HID, DIM), BF16),
        ),
        in_specs=[pl.BlockSpec(memory_space=pltpu.HBM)] * 5,
        out_specs=(pl.BlockSpec(memory_space=pltpu.VMEM),) * 4,
        scratch_shapes=[
            vmem((IMG * TOK, DIM), BF16),
            vmem((IMG * TOK, DIM), BF16),
            vmem((EXP, DIM), BF16),
            vmem((EXP, DIM), BF16),
            vmem((DIM, HID), BF16),
            vmem((HID, DIM), BF16),
            vmem((256, 1024), BF16),
            vmem((IMG * TOK, EXP), F32),
            vmem((IMG * TOK, EXP), F32),
            vmem((IMG * TOK, EXP), BF16),
            vmem((128, 128), BF16),
            vmem((128, 128), BF16),
            vmem((UNITS, 128, CW), BF16),
            vmem((UNITS, 128, CW), BF16),
            vmem((UNITS, 2, 64, CW), BF16),
            vmem((UNITS, N_BLK, 2, 64, CW), BF16),
            vmem((2, 256, HID), F32),
            vmem((2, 256, HID), F32),
            vmem((2, 256, HID), BF16),
            vmem((2, 256, HID), BF16),
            vmem((UNITS, N_BLK, 2, 64, CW), BF16),
            vmem((UNITS, 2, 2, 64, CW), BF16),
            vmem((UNITS, 2, 64, CW), F32),
            vmem((UNITS, 2, 64, CW), BF16),
            vmem((UNITS, 2, 64, CW), BF16),
            vmem((UNITS, 2, 64, CW), BF16),
            vmem((UNITS, 2, 64, CW), BF16),
            vmem((UNITS, 128, CW), BF16),
            vmem((UNITS, 128, CW), BF16),
            vmem((2, 128, DIM), BF16),
            vmem((2, IMG * TOK, EXP), F32),
            vmem((2, IMG * TOK, EXP), F32),
            vmem((IMG * TOK, 2 * EXP), BF16),
            vmem((NZ * 16, HID), BF16),
            vmem((NZ * 16, HID), BF16),
            vmem((NYX, 2, HID), F32),
            vmem((NYX, 2, HID), F32),
            vmem((2, HID), F32),
            vmem((4, 2, HID), F32),
            dma((5,)),
            dma((UNITS,)), dma((UNITS,)), dma((UNITS,)), dma((UNITS,)), dma((UNITS,)),
            dma((UNITS,)), dma((UNITS,)), dma((UNITS,)), dma((UNITS,)),
            dma((3,)), dma((12,)),
        ],
        compiler_params=pltpu.CompilerParams(
            collective_id=0, has_side_effects=True, vmem_limit_bytes=56 * 1024 * 1024
        ),
    )(
        tokens.reshape(IMG * TOK, DIM), cotangent.reshape(IMG * TOK, DIM), router.T,
        first_weight[0], second_weight[0],
    )
    token_grad, router_column, first_grad, second_grad = pl.pallas_call(
        store_kernel,
        out_shape=(
            jax.ShapeDtypeStruct((IMG * TOK, DIM), BF16),
            jax.ShapeDtypeStruct((1, DIM), F32),
            jax.ShapeDtypeStruct((DIM, HID), BF16),
            jax.ShapeDtypeStruct((HID, DIM), BF16),
        ),
        in_specs=[pl.BlockSpec(memory_space=pltpu.VMEM)] * 4,
        out_specs=(
            pl.BlockSpec(memory_space=pl.ANY),
            pl.BlockSpec(memory_space=pltpu.VMEM),
            pl.BlockSpec(memory_space=pl.ANY),
            pl.BlockSpec(memory_space=pl.ANY),
        ),
        scratch_shapes=[dma((3,))],
        compiler_params=pltpu.CompilerParams(vmem_limit_bytes=8 * 1024 * 1024),
    )(*results)
    return (
        token_grad.reshape(IMG, TOK, DIM),
        router_column.reshape(DIM, 1),
        first_grad[None],
        second_grad[None],
    )


def solution(mesh):
    placed = (
        P(("dp", "expert"), None, None),
        P(("dp", "expert"), None, None),
        P(),
        P("expert", None, "dp"),
        P("expert", "dp", None),
    )
    return jax.shard_map(
        body,
        mesh=mesh,
        in_specs=placed,
        out_specs=(
            P(("dp", "expert"), None, None),
            P(None, "expert"),
            P("expert", None, "dp"),
            P("expert", "dp", None),
        ),
        check_vma=False,
    )
```

time: 92.9 us -> 81.6 us (0.88)
  Pallas kernels: 92.2 us -> 80.6 us
    pallas_call x1, Pallas kernels: 89.5 us -> 77.8 us  [body(): pl.pallas_call(kernel, out_shape=(vmem((IMG * TOK, DIM), BF16), vmem((2,...]
where the time goes in v4:
time: 81.6 us; the launch traced here: 81.2 us
  Pallas kernels  80.6 us (99%)
    pallas_call x1, Pallas kernels, body(): pl.pallas_call(kernel, out_shape=(vmem((IMG * TOK, DIM), BF16), vmem((2,...  77.8 us
    pallas_call x1, Pallas kernels, body(): pl.pallas_call(store_kernel, out_shape=(jax.ShapeDtypeStruct((IMG * TOK,...  2.76 us

profile of v4, /device:TPU:1, one launch (start us, length us, event | category | flops | bytes accessed | tf_op | source)
XLA Modules:
  0.0 81.2 jit_solution(14464649377753723703)
XLA Ops:
  0.6 77.8 %shard_map.84 = (bf16[512,1280]{1,0:T(8,128)(2,1)S(1)}, f32[2,640]{1,0:T(2,128)S(1)}, bf16[1280,640]{1,0:T(8,128)(2,1)S(1)}, bf16[640,1280]{1,0:T(8,128)(2,1)S(1)}) custom-call(bf16[512,1280]{1,0:T(8,128)(2,1)} %bitcast.11, bf16[512,1280]{1,0:T(8,128)(2,1)} %bitcast.12, bf16[64,1280]{1,0:T(8,128)(2,1)} %bitcast.13, bf16[1280,640]{1,0:T(8,128)(2,1)} %bitcast.9, ...), custom_call_target="tpu_custom_call" | custom-call | tf_op jit(solution)/shard_map/pallas_call | solution.py:371
  78.5 2.8 %shard_map.85 = (bf16[512,1280]{1,0:T(8,128)(2,1)}, f32[1,1280]{1,0:T(1,128)}, bf16[1280,640]{1,0:T(8,128)(2,1)}, bf16[640,1280]{1,0:T(8,128)(2,1)}) custom-call(bf16[512,1280]{1,0:T(8,128)(2,1)S(1)} %get-tuple-element.12.tg, f32[2,640]{1,0:T(2,128)S(1)} %get-tuple-element.13.rg, bf16[1280,640]{1,0:T(8,128)(2,1)S(1)} %get-tuple-element.14.g1, ...), custom_call_target="tpu_custom_call" | custom-call | tf_op jit(solution)/shard_map/pallas_call | solution.py:433

commit v5 on v4

--- a/solution.py
+++ b/solution.py
@@ -47,8 +47,8 @@
     tok, cot, rt, rtj, w1, w2, ltm, disp, comb, dlow, perm1, perm3,
     send1, recv1, send2, xs, acc_pre, acc_act, hid, pg,
     op, rc, t_own, sx, rx, so, ry, sz, rz, rp, cgx, dgx, low2,
-    rsend, rrecv, rs2, rr2, rs3, rr3,
-    in_sem, z1_sem, y1_sem, agx_sem, agc_sem, agd_sem,
+    rsend, rrecv, rs2, rr2, rr3,
+    in_sem, z1_sem, y1_sem, agx_sem, agc_sem,
     rc_sem, rx_sem, ry_sem, rz_sem, rt_sem, snd_sem,
 ):
     p = lax.axis_index("dp")
@@ -58,7 +58,7 @@
     y = lax.div(yx, 2)
     xh = lax.rem(yx, 2)
 
-    z_at = [lax.rem(z + far, NZ) for far in (1, 7, 2, 6, 3, 5, 4)]
+    z_at = [lax.rem(z + far, NZ) for far in (4, 3, 5, 2, 6, 1, 7)]
     z_peers = [(zt, (p, yx * NZ + zt)) for zt in z_at]
     p_flip = lax.rem(p + 2, 4)
     p_at, xh_at = (p, p_flip), (xh, 1 - xh)
@@ -99,7 +99,8 @@
 
     barrier = pltpu.get_barrier_semaphore()
 
-    for dev in [dev for _, dev in z_peers + yx_peers] + dp_peers:
+    column = [(pt, yx * NZ + zt) for zt in z_at for pt, _ in dp_peers]
+    for dev in [dev for _, dev in z_peers + yx_peers] + dp_peers + column:
         pl.semaphore_signal(barrier, inc=1, device_id=dev, device_id_type=MESH)
 
     o1, n1 = iota((128, 128), 0), iota((128, 128), 1)
@@ -137,7 +138,7 @@
             spread = one_hot(same_slot & ((n2 & 3) == a * 2 + i))
             ltm[:, pl.ds(a * 512 + i * TOK, TOK)] = mm_nt(spread, low).astype(BF16)
     loads[2].wait()
-    pl.semaphore_wait(barrier, 17)
+    pl.semaphore_wait(barrier, 38)
 
     def send_slots(u):
         h, c, ch = split(u)
@@ -155,10 +156,6 @@
             )
 
     def to_neighbours(h, src, dst, send_sem, recv_sem, sign):
-        @pl.when(h == 0)
-        def _():
-            pltpu.make_async_copy(src(0), dst(0), recv_sem).start()
-
         @pl.when(h == 1)
         def _():
             remote(src(0), dst(0), send_sem, recv_sem, yx_peer(2, 0)[1])
@@ -167,10 +164,24 @@
         for k in range(1, 4):
             remote(src(k), dst(k), send_sem, recv_sem, yx_peer(start + sign * (k // 2), k % 2)[1])
 
+    def await_neighbours(h, ref, sem):
+        @pl.when(h == 0)
+        def _():
+            await_bytes(ref.at[:, pl.ds(0, 48)], sem)
+
+        @pl.when(h == 1)
+        def _():
+            await_bytes(ref, sem)
+
     def turn_slots(u):
         h, c, ch = split(u)
         await_bytes(recv1.at[u, pl.ds(0, 112)], z1_sem.at[u])
         send2[u] = mm(perm1[...], recv1[u]).astype(BF16).reshape(2, 64, CW)
+
+        @pl.when(h == 0)
+        def _():
+            xs[u, 0, :, :16] = send2[u, :, :16]
+
         to_neighbours(
             h, lambda k: send2.at[u, :, rows_at(k, 16)],
             lambda k: xs.at[u, 0, :, rows_at(k, 16)], snd_sem.at[1], y1_sem.at[u], 1,
@@ -178,19 +189,19 @@
 
     def gather_slots(u):
         h, c, ch = split(u)
-        await_bytes(xs.at[u, 0], y1_sem.at[u])
+        await_neighbours(h, xs.at[u, 0], y1_sem.at[u])
         remote(xs.at[u, 0], xs.at[u, 1], snd_sem.at[2], agx_sem.at[u], x_peer)
-        remote(xs.at[u, 0], xs.at[u, 2], snd_sem.at[3], agc_sem.at[u], core_peer)
 
     def forward_slots(u):
         h, c, ch = split(u)
         await_bytes(xs.at[u, 1], agx_sem.at[u])
-        remote(xs.at[u, 1], xs.at[u, 3], snd_sem.at[4], agd_sem.at[u], core_peer)
+        remote(
+            xs.at[u, pl.ds(0, 2)], xs.at[u, pl.ds(2, 2)], snd_sem.at[3], agc_sem.at[u], core_peer
+        )
 
     def first_layer(u):
         h, c, ch = split(u)
-        await_bytes(xs.at[u, 2], agc_sem.at[u])
-        await_bytes(xs.at[u, 3], agd_sem.at[u])
+        await_bytes(xs.at[u, pl.ds(2, 2)], agc_sem.at[u])
         acc_pre[h] += mm(xs[u, :, 0].reshape(256, CW), w1[ch, :])
         acc_act[h] += mm_nt(xs[u, :, 1].reshape(256, CW), w2[:, ch])
 
@@ -241,6 +252,11 @@
         h, c, ch = split(u)
         await_bytes(rx.at[u], rx_sem.at[u])
         so[u] = (t_own[u] + rx[u].astype(F32)).astype(BF16)
+
+        @pl.when(h == 0)
+        def _():
+            ry[u, :, :16] = so[u, :, :16]
+
         to_neighbours(
             h, lambda k: so.at[u, :, rows_at(k, 16)],
             lambda k: ry.at[u, :, rows_at(k, 16)], snd_sem.at[7], ry_sem.at[u], -1,
@@ -248,7 +264,7 @@
 
     def turn_back(u):
         h, c, ch = split(u)
-        await_bytes(ry.at[u], ry_sem.at[u])
+        await_neighbours(h, ry.at[u], ry_sem.at[u])
         sz[u] = mm_tn(perm1[...], ry[u].reshape(128, CW)).astype(BF16)
         mine = rows_at(z, 16)
         rz[u, mine] = sz[u, mine]
@@ -273,8 +289,8 @@
     def _(step):
         for lag, count, stage in (
             (0, UNITS, send_slots), (16, UNITS, second_layer), (23, UNITS, turn_back),
-            (7, UNITS, gather_slots), (20, UNITS, x_sum), (31, NC, weight_grads),
-            (4, UNITS, turn_slots), (28, UNITS, slots_back), (10, UNITS, forward_slots),
+            (7, UNITS, gather_slots), (20, UNITS, x_sum), (4, UNITS, turn_slots),
+            (28, UNITS, slots_back), (31, NC, weight_grads), (10, UNITS, forward_slots),
             (17, UNITS, core_sum), (11, UNITS, first_layer),
         ):
             @pl.when((step >= lag) & (step < lag + count))
@@ -299,20 +315,35 @@
         low2[rows, :64] = dlow[rows, :]
         low2[rows, 64:] = grad.astype(BF16)
 
-    e3, j3 = iota((EXP, EXP), 1), iota((EXP, EXP), 0)
-    by_z = one_hot(expert_of(j3) == (e3 & 7) * 8 + (e3 >> 3))
-    turned = mm(low2[:, 64:], by_z).astype(BF16)
+    all_but_one = rr3.at[pl.ds(0, 31)]
+
+    r3, j3 = iota((EXP, EXP), 1), iota((EXP, EXP), 0)
+    by_peer = one_hot(j3 == (r3 >> 5) * 32 + (r3 & 7) * 4 + ((r3 >> 3) & 3))
+    turned = mm(low2[:, 64:], by_peer).astype(BF16)
     part = mm_tn(turned, tok[...])
-    for k in range(NZ):
+    for k in range(NYX):
         rows = part[k * 8:(k + 1) * 8]
         rsend[pl.ds(k * 16, 16), :] = jnp.concatenate(
             [rows[:, :HID], rows[:, HID:]], axis=0
         ).astype(BF16)
-    mine_z = rows_at(z, 16)
-    pltpu.make_async_copy(rsend.at[mine_z], rrecv.at[mine_z], rt_sem.at[0]).start()
-
-    for zt, dev in z_peers:
-        remote(rsend.at[rows_at(zt, 16)], rrecv.at[mine_z], snd_sem.at[9], rt_sem.at[0], dev)
+    for k, (_, dev) in enumerate(yx_peers, 1):
+        rows = pl.ds(k * 16, 16)
+        remote(rsend.at[rows], rrecv.at[rows], snd_sem.at[9], rt_sem.at[0], dev)
+
+    await_bytes(rrecv.at[pl.ds(16, 112)], rt_sem.at[0])
+    total = rsend[pl.ds(0, 16), :].astype(F32)
+    for k in range(1, NYX):
+        total = total + rrecv[pl.ds(k * 16, 16), :].astype(F32)
+    for k in range(NZ):
+        rs2[k, pl.ds(0, 1), :] = total[k:k + 1]
+        rs2[k, pl.ds(1, 1), :] = total[8 + k:9 + k]
+    for zt in [z] + z_at:
+        for pt in [p] + [pt for pt, _ in dp_peers]:
+            if zt is not z or pt is not p:
+                remote(
+                    rs2.at[zt], rr2.at[p, z], snd_sem.at[10], rt_sem.at[1], (pt, yx * NZ + zt)
+                )
+    rr2[p, z] = rs2[z]
 
     for i in range(IMG):
         rows = pl.ds(i * TOK, TOK)
@@ -324,31 +355,15 @@
             right = jnp.concatenate([rp[0, back, ch], rp[1, back, ch], rtj[:, ch]], axis=0)
             tgv[rows, ch] = mm(low2[rows, :], right).astype(BF16)
 
-    await_bytes(rrecv, rt_sem.at[0])
-    total = rrecv[pl.ds(0, 16), :].astype(F32)
-    for k in range(1, NZ):
-        total = total + rrecv[pl.ds(k * 16, 16), :].astype(F32)
-    for k in range(NYX):
-        rs2[k, pl.ds(0, 1), :] = total[k:k + 1]
-        rs2[k, pl.ds(1, 1), :] = total[8 + k:9 + k]
-    pltpu.make_async_copy(rs2.at[yx], rr2.at[yx], rt_sem.at[1]).start()
-
-    for yxt, dev in yx_peers:
-        remote(rs2.at[yxt], rr2.at[yx], snd_sem.at[10], rt_sem.at[1], dev)
-
-    await_bytes(rr2, rt_sem.at[1])
-    rs3[...] = jnp.sum(rr2[...], axis=0)
-    pltpu.make_async_copy(rs3, rr3.at[p], rt_sem.at[2]).start()
-    for dev in dp_peers:
-        remote(rs3, rr3.at[p], snd_sem.at[11], rt_sem.at[2], dev)
-    await_bytes(rr3, rt_sem.at[2])
-    rg_out[...] = (rr3[0] + rr3[1]) + (rr3[2] + rr3[3])
+    await_bytes(all_but_one, rt_sem.at[1])
+    sums = [jnp.sum(rr2[k], axis=0) for k in range(4)]
+    rg_out[...] = (sums[0] + sums[1]) + (sums[2] + sums[3])
 
     seven = send1.at[:, pl.ds(0, 112)]
     for ref, number in (
-        (seven, 0), (seven, 1), (xs.at[:, 0], 2), (xs.at[:, 0], 3), (xs.at[:, 1], 4),
+        (seven, 0), (seven, 1), (xs.at[:, 0], 2), (xs.at[:, pl.ds(0, 2)], 3),
         (rc, 5), (sx, 6), (seven, 7), (seven, 8),
-        (rsend.at[pl.ds(0, 112)], 9), (rs2.at[pl.ds(0, 7)], 10), (rr3.at[pl.ds(0, 3)], 11),
+        (rsend.at[pl.ds(0, 112)], 9), (all_but_one, 10),
     ):
         await_bytes(ref, snd_sem.at[number])
 
@@ -415,11 +430,10 @@
             vmem((NZ * 16, HID), BF16),
             vmem((NZ * 16, HID), BF16),
             vmem((NYX, 2, HID), F32),
-            vmem((NYX, 2, HID), F32),
-            vmem((2, HID), F32),
-            vmem((4, 2, HID), F32),
+            vmem((4, NZ, 2, HID), F32),
+            vmem((32, 2, HID), F32),
             dma((5,)),
-            dma((UNITS,)), dma((UNITS,)), dma((UNITS,)), dma((UNITS,)), dma((UNITS,)),
+            dma((UNITS,)), dma((UNITS,)), dma((UNITS,)), dma((UNITS,)),
             dma((UNITS,)), dma((UNITS,)), dma((UNITS,)), dma((UNITS,)),
             dma((3,)), dma((12,)),
         ],

time: 81.6 us -> 79.3 us (0.972)
  Pallas kernels: 80.6 us -> 78.5 us
    pallas_call x1, Pallas kernels: 77.8 us -> 75.8 us  [body(): pl.pallas_call(kernel, out_shape=(vmem((IMG * TOK, DIM), BF16), vmem((2,...]
where the time goes in v5:
time: 79.3 us; the launch traced here: 79.1 us
  Pallas kernels  78.5 us (99%)
    pallas_call x1, Pallas kernels, body(): pl.pallas_call(kernel, out_shape=(vmem((IMG * TOK, DIM), BF16), vmem((2,...  75.8 us
    pallas_call x1, Pallas kernels, body(): pl.pallas_call(store_kernel, out_shape=(jax.ShapeDtypeStruct((IMG * TOK,...  2.76 us

profile of v5, /device:TPU:1, one launch (start us, length us, event | category | flops | bytes accessed | tf_op | source)
XLA Modules:
  0.0 79.1 jit_solution(2344443353592883632)
XLA Ops:
  0.6 75.8 %shard_map.84 = (bf16[512,1280]{1,0:T(8,128)(2,1)S(1)}, f32[2,640]{1,0:T(2,128)S(1)}, bf16[1280,640]{1,0:T(8,128)(2,1)S(1)}, bf16[640,1280]{1,0:T(8,128)(2,1)S(1)}) custom-call(bf16[512,1280]{1,0:T(8,128)(2,1)} %bitcast.11, bf16[512,1280]{1,0:T(8,128)(2,1)} %bitcast.12, bf16[64,1280]{1,0:T(8,128)(2,1)} %bitcast.13, bf16[1280,640]{1,0:T(8,128)(2,1)} %bitcast.9, ...), custom_call_target="tpu_custom_call" | custom-call | tf_op jit(solution)/shard_map/pallas_call | solution.py:386
  76.4 2.8 %shard_map.85 = (bf16[512,1280]{1,0:T(8,128)(2,1)}, f32[1,1280]{1,0:T(1,128)}, bf16[1280,640]{1,0:T(8,128)(2,1)}, bf16[640,1280]{1,0:T(8,128)(2,1)}) custom-call(bf16[512,1280]{1,0:T(8,128)(2,1)S(1)} %get-tuple-element.12.tg, f32[2,640]{1,0:T(2,128)S(1)} %get-tuple-element.13.rg, bf16[1280,640]{1,0:T(8,128)(2,1)S(1)} %get-tuple-element.14.g1, ...), custom_call_target="tpu_custom_call" | custom-call | tf_op jit(solution)/shard_map/pallas_call | solution.py:447

commit v6 on v5

--- a/solution.py
+++ b/solution.py
@@ -161,7 +161,7 @@
             remote(src(0), dst(0), send_sem, recv_sem, yx_peer(2, 0)[1])
 
         start = 2 * h if sign > 0 else 8 - 2 * h
-        for k in range(1, 4):
+        for k in (3, 2, 1):
             remote(src(k), dst(k), send_sem, recv_sem, yx_peer(start + sign * (k // 2), k % 2)[1])
 
     def await_neighbours(h, ref, sem):
@@ -326,7 +326,8 @@
         rsend[pl.ds(k * 16, 16), :] = jnp.concatenate(
             [rows[:, :HID], rows[:, HID:]], axis=0
         ).astype(BF16)
-    for k, (_, dev) in enumerate(yx_peers, 1):
+    for k in (5, 4, 3, 7, 2, 6, 1):
+        dev = yx_peers[k - 1][1]
         rows = pl.ds(k * 16, 16)
         remote(rsend.at[rows], rrecv.at[rows], snd_sem.at[9], rt_sem.at[0], dev)
 
@@ -337,8 +338,8 @@
     for k in range(NZ):
         rs2[k, pl.ds(0, 1), :] = total[k:k + 1]
         rs2[k, pl.ds(1, 1), :] = total[8 + k:9 + k]
-    for zt in [z] + z_at:
-        for pt in [p] + [pt for pt, _ in dp_peers]:
+    for zt in z_at + [z]:
+        for pt in [pt for pt, _ in dp_peers] + [p]:
             if zt is not z or pt is not p:
                 remote(
                     rs2.at[zt], rr2.at[p, z], snd_sem.at[10], rt_sem.at[1], (pt, yx * NZ + zt)

time: 79.3 us -> 78.9 us (level)
  no operation moved by 1% of the time
where the time goes in v6:
time: 78.9 us; the launch traced here: 78.8 us
  Pallas kernels  78.2 us (99%)
    pallas_call x1, Pallas kernels, body(): pl.pallas_call(kernel, out_shape=(vmem((IMG * TOK, DIM), BF16), vmem((2,...  75.4 us
    pallas_call x1, Pallas kernels, body(): pl.pallas_call(store_kernel, out_shape=(jax.ShapeDtypeStruct((IMG * TOK,...  2.76 us

profile of v6, /device:TPU:1, one launch (start us, length us, event | category | flops | bytes accessed | tf_op | source)
XLA Modules:
  0.0 78.8 jit_solution(17459236396716369925)
XLA Ops:
  0.6 75.4 %shard_map.84 = (bf16[512,1280]{1,0:T(8,128)(2,1)S(1)}, f32[2,640]{1,0:T(2,128)S(1)}, bf16[1280,640]{1,0:T(8,128)(2,1)S(1)}, bf16[640,1280]{1,0:T(8,128)(2,1)S(1)}) custom-call(bf16[512,1280]{1,0:T(8,128)(2,1)} %bitcast.11, bf16[512,1280]{1,0:T(8,128)(2,1)} %bitcast.12, bf16[64,1280]{1,0:T(8,128)(2,1)} %bitcast.13, bf16[1280,640]{1,0:T(8,128)(2,1)} %bitcast.9, ...), custom_call_target="tpu_custom_call" | custom-call | tf_op jit(solution)/shard_map/pallas_call | solution.py:387
  76.1 2.8 %shard_map.85 = (bf16[512,1280]{1,0:T(8,128)(2,1)}, f32[1,1280]{1,0:T(1,128)}, bf16[1280,640]{1,0:T(8,128)(2,1)}, bf16[640,1280]{1,0:T(8,128)(2,1)}) custom-call(bf16[512,1280]{1,0:T(8,128)(2,1)S(1)} %get-tuple-element.12.tg, f32[2,640]{1,0:T(2,128)S(1)} %get-tuple-element.13.rg, bf16[1280,640]{1,0:T(8,128)(2,1)S(1)} %get-tuple-element.14.g1, ...), custom_call_target="tpu_custom_call" | custom-call | tf_op jit(solution)/shard_map/pallas_call | solution.py:448
